TPU v7x, 128 devices: a whole 4x4x4 slice. The times are simulated.
128 devices in a mesh: fsdp: 32 (over y, z, core), rep: 4 (over x).
Axes of the slice: x: 4, y: 4, z: 4, core: 2. Of those that a mesh axis runs over, the one named last changes fastest.
Arguments:
- grad_partial: bfloat16 [4, 32, 1024, 1024], P('rep', None, 'fsdp'), may hold values from -52 to 52
- second_moment: float32 [32, 1024, 1024], P(None, 'fsdp', 'rep'), may hold values from 0.02 to 150
- left_factor: bfloat16 [96, 1024, 1024], P('fsdp'), may hold values from -0.6 to 2.6
- right_factor: bfloat16 [96, 1024, 1024], P('fsdp'), may hold values from -0.6 to 2.6
- block_owner: int32 [32], replicated, may hold values from 0 to 31, as said below
- block_slot: int32 [32], replicated, may hold values from 0 to 2, as said below
Outputs:
- update: bfloat16 [32, 1024, 1024], P(None, 'fsdp', 'rep')
- new_moment: float32 [32, 1024, 1024], P(None, 'fsdp', 'rep')
Inputs may be any that keep to these rules, and one draw needn't show every extreme that they name: `block_owner`: each device owns at most 3 blocks, and some device owns exactly 3. `block_slot`: no two blocks share an owner and a slot; a device that owns c blocks holds them at slots 0 to c - 1; the factors of the block at owner d, slot s are entry d * 3 + s of left_factor and right_factor.
All inputs are finite; a program needn't handle non-finite values.
Results may differ from a plain program's by a relative error of at most 0.017.
Values may be sent and summed in bfloat16 or wider, within the bound.
A program may use at most 128 MiB of HBM per device.

v0:
```python
import jax
import jax.numpy as jnp
from jax import lax
from jax.sharding import PartitionSpec as P


def per_device(grad_partial, second_moment, left_factor, right_factor, block_owner, block_slot):
    slot_count = left_factor.shape[0]
    row_count = grad_partial.shape[2]
    full_width = grad_partial.shape[3]
    rep_count = lax.axis_size("rep")
    owner_count = lax.axis_size("fsdp")
    owner_index = lax.axis_index("fsdp")
    rep_index = lax.axis_index("rep")
    quarter = full_width // rep_count
    slot_range = jnp.arange(slot_count, dtype=jnp.int32)
    owner_range = jnp.arange(owner_count, dtype=jnp.int32)
    selector = (
        (block_slot[None, None, :] == slot_range[:, None, None])
        & (block_owner[None, None, :] == owner_range[None, :, None])
    ).astype(jnp.bfloat16)
    owned = (
        (block_slot[None, :] == slot_range[:, None]) & (block_owner[None, :] == owner_index)
    ).astype(jnp.float32)
    local_grad = grad_partial[0].astype(jnp.float32)
    summed = lax.psum(local_grad.astype(jnp.bfloat16), "rep").astype(jnp.float32)
    column = lax.dynamic_slice_in_dim(summed, rep_index * quarter, quarter, 2)
    new_moment = 0.99 * second_moment + 0.01 * column * column
    adam = column / (jnp.sqrt(new_moment) + 1e-08)
    partial_squares = jnp.sum(adam * adam, axis=(1, 2))
    total_squares = lax.psum(partial_squares, ("fsdp", "rep"))
    adam_rms = jnp.sqrt(total_squares / (full_width * full_width))
    slot_rms = jnp.sum(owned * adam_rms[None, :], axis=1)
    grad_bf = summed.astype(jnp.bfloat16)
    outbound = jnp.einsum(
        "kdn,nrc->kdrc", selector, grad_bf, preferred_element_type=jnp.float32
    ).astype(jnp.bfloat16)
    outbound = outbound.reshape(slot_count, owner_count * row_count, full_width)
    inbound = lax.all_to_all(outbound, "fsdp", split_axis=1, concat_axis=1, tiled=True)
    left_prod = jnp.einsum(
        "kij,kjc->kic", left_factor, inbound, preferred_element_type=jnp.float32
    ).astype(jnp.bfloat16)
    product = jnp.einsum(
        "kij,kjc->kic", left_prod, right_factor, preferred_element_type=jnp.float32
    )
    prod_mean = jnp.mean(product * product, axis=(1, 2))
    graft = slot_rms / jnp.sqrt(prod_mean + 1e-06)
    scaled = (product * graft[:, None, None]).astype(jnp.bfloat16)
    returned = lax.all_to_all(scaled, "fsdp", split_axis=1, concat_axis=1, tiled=True)
    returned = lax.dynamic_slice_in_dim(returned, rep_index * quarter, quarter, 2)
    returned = returned.reshape(slot_count, owner_count, row_count, quarter)
    update = jnp.einsum(
        "kdn,kdrc->nrc", selector, returned, preferred_element_type=jnp.float32
    ).astype(jnp.bfloat16)
    return (update, new_moment)


def solution(mesh):
    placed = (
        P("rep", None, "fsdp", None),
        P(None, "fsdp", "rep"),
        P("fsdp", None, None),
        P("fsdp", None, None),
        P(),
        P(),
    )
    return jax.shard_map(
        per_device,
        mesh=mesh,
        in_specs=placed,
        out_specs=(P(None, "fsdp", "rep"), P(None, "fsdp", "rep")),
        check_vma=False,
    )
```

profile of v0, /device:TPU:48, one launch (start us, length us, event | category | flops | bytes accessed | tf_op | source)
XLA Modules:
  0.0 467.8 jit_solution(14659366554377348112)
XLA Ops:
  7.2 0.0 copy-start.2
  7.2 0.0 copy-start.1
  7.2 0.0 all-reduce.2.cloned.1.call-start
  7.2 4.1 copy.57
  11.3 0.0 all-reduce.2.cloned.1.call-update
  11.3 0.0 copy-done.2
  11.4 0.0 copy-done.1
  11.4 0.1 iota_compare_fusion
  11.5 60.5 %all-reduce.2.cloned.1.call-done = bf16[32,32,1024]{2,0,1:T(8,128)(2,1)} async-done(((bf16[32,32,1024]{2,0,1:T(8,128)(2,1)}), bf16[32,32,1024]{2,0,1:T(8,128)(2,1)}) %all-reduce.2.cloned.1.call-update) | async-done | bytes 2097168 | tf_op jit(solution)/shard_map/psum | solution.py:26
  72.0 3.5 convolution_convert_fusion
  75.5 6.3 %copy.22 = bf16[3,32,32,1024]{3,2,1,0:T(8,128)(2,1)} copy(bf16[3,32,32,1024]{3,1,2,0:T(8,128)(2,1)S(1)} %convolution_convert_fusion) | data formatting | bytes 12582912 | tf_op jit(solution)/shard_map/convert_element_type | solution.py:37
  81.7 11.6 %copy.23 = bf16[3,1024,1024]{2,0,1:T(4,128)(2,1)} copy(bf16[3,1024,1024]{2,1,0:T(8,128)(2,1)} %bitcast.23) | data formatting | bytes 12582912 | tf_op jit(solution)/shard_map/reshape | solution.py:38
  93.3 0.0 copy-start
  93.3 7.7 %all-to-all-start = ((bf16[3,1024,1024]{2,0,1:T(4,128)(2,1)}), bf16[3,1024,1024]{2,0,1:T(4,128)(2,1)}, u32[]{:S(2)}, u32[]{:S(2)}) async-start(bf16[3,1024,1024]{2,0,1:T(4,128)(2,1)} %copy.23), calls=%async_computation | async-start | bytes 16777216 | tf_op jit(solution)/shard_map/all_to_all | solution.py:39
  101.0 0.0 copy-done
  101.0 2.0 fusion.19
  103.0 173.5 %psum.15 = f32[32]{0:T(128)S(1)} all-reduce(f32[32]{0:T(128)S(1)} %get-tuple-element.8), channel_id=1, replica_groups=mesh['fsdp'=32,'rep'=4] {'fsdp','rep'}, use_global_device_ids=true, to_apply=%region_2.0 | all-reduce | flops 32 | bytes 256 | tf_op jit(solution)/shard_map/psum | solution.py:31
  276.6 0.1 select_reduce_fusion
  276.7 0.0 all-to-all-done
  276.7 27.5 %multiply_reduce_fusion = (f32[3]{0:T(128)S(1)}, f32[3,1024,1024]{2,1,0:T(8,128)}) fusion(bf16[3,1024,1024]{2,1,0:T(8,128)(2,1)} %param.9, bf16[3,1024,1024]{2,1,0:T(8,128)(2,1)} %param.8, bf16[3,1024,1024]{2,0,1:T(4,128)(2,1)} %all-to-all-done), kind=kOutput, calls=%fused_computation.1 | convolution fusion | flops 12894339072 | bytes 31457292 | tf_op jit(solution)/shard_map/kij,kjc->kic/dot_general | solution.py:43
  304.2 9.2 %multiply_convert_fusion = bf16[3,1024,1024]{2,1,0:T(8,128)(2,1)} fusion(f32[3,1024,1024]{2,1,0:T(8,128)} %get-tuple-element.11, f32[3]{0:T(128)S(1)} %rsqrt_multiply_fusion), kind=kLoop, calls=%fused_computation | loop fusion | flops 6291456 | bytes 18874380 | tf_op jit(solution)/shard_map/convert_element_type | solution.py:48
  313.3 11.4 %copy.27 = bf16[3,1024,1024]{2,0,1:T(4,128)(2,1)} copy(bf16[3,1024,1024]{2,1,0:T(8,128)(2,1)} %multiply_convert_fusion) | data formatting | bytes 12582912 | tf_op jit(solution)/shard_map/convert_element_type | solution.py:48
  324.7 7.1 %all-to-all-start.1 = ((bf16[3,1024,1024]{2,0,1:T(4,128)(2,1)}), bf16[3,1024,1024]{2,0,1:T(4,128)(2,1)}, u32[]{:S(2)}, u32[]{:S(2)}) async-start(bf16[3,1024,1024]{2,0,1:T(4,128)(2,1)} %copy.27), calls=%async_computation.1 | async-start | bytes 16777216 | tf_op jit(solution)/shard_map/all_to_all | solution.py:49
  331.9 1.6 copy.31
  333.5 122.7 %all-to-all-done.1 = bf16[3,1024,1024]{2,0,1:T(4,128)(2,1)} async-done(((bf16[3,1024,1024]{2,0,1:T(4,128)(2,1)}), bf16[3,1024,1024]{2,0,1:T(4,128)(2,1)}, u32[]{:S(2)}, u32[]{:S(2)}) %all-to-all-start.1) | async-done | bytes 6291488 | tf_op jit(solution)/shard_map/all_to_all | solution.py:49
  456.2 2.3 constant_dynamic-slice_fusion
  458.5 0.2 copy.37
  458.7 1.1 fusion.14
  459.8 1.1 copy.30
  (4 shorter events, 0.0 us)
Async XLA Ops:
  7.2 4.2 copy-start.2
  7.2 4.2 copy-start.1
  7.2 64.8 %all-reduce.2.cloned.1.call-start = ((), (), s32[]{:S(2)}) async-start(), calls=%async_computation.2 | async-start | bytes 4194304 | tf_op jit(solution)/shard_map/psum | solution.py:26
  93.3 7.7 %copy-start = (f32[32,32,256]{2,1,0:T(8,128)S(1)}, f32[32,32,256]{2,1,0:T(8,128)}, u32[]{:S(2)}) copy-start(f32[32,32,256]{2,1,0:T(8,128)} %param.7) | copy-start | bytes 3145732
  93.3 183.4 %all-to-all-start = ((bf16[3,1024,1024]{2,0,1:T(4,128)(2,1)}), bf16[3,1024,1024]{2,0,1:T(4,128)(2,1)}, u32[]{:S(2)}, u32[]{:S(2)}) async-start(bf16[3,1024,1024]{2,0,1:T(4,128)(2,1)} %copy.23), calls=%async_computation | async-start | bytes 16777216 | tf_op jit(solution)/shard_map/all_to_all | solution.py:39
  324.7 131.4 %all-to-all-start.1 = ((bf16[3,1024,1024]{2,0,1:T(4,128)(2,1)}), bf16[3,1024,1024]{2,0,1:T(4,128)(2,1)}, u32[]{:S(2)}, u32[]{:S(2)}) async-start(bf16[3,1024,1024]{2,0,1:T(4,128)(2,1)} %copy.27), calls=%async_computation.1 | async-start | bytes 16777216 | tf_op jit(solution)/shard_map/all_to_all | solution.py:49
Sparse Core Ops, SparseCore 0:
  11.5 60.4 all-reduce.1
where the time goes:
time: 468 us
  waiting for transfers between devices  183 us (39%)
  blocking collectives  174 us (37%)
  local copies, waits for them, and re-layouts  38.5 us (8%)
  matrix products  32.1 us (7%)
  starting transfers between devices  14.8 us (3%)
  between operations  14.1 us (3%)
  other arithmetic  11.4 us (2%)
    psum x1, blocking collectives, per_device(): total_squares = lax.psum(partial_squares, ('fsdp', 'rep'))  174 us
    all_to_all x1, waiting for transfers between devices, per_device(): lax.all_to_all(scaled, 'fsdp', split_axis=1, concat_axis=1, tiled=True)  123 us
    psum x1, waiting for transfers between devices, per_device(): lax.psum(local_grad.astype(jnp.bfloat16), 'rep').astype(jnp.float32)  60.5 us
    dot_general x1, matrix products, per_device(): jnp.einsum('kij,kjc->kic', left_prod, right_factor, preferred_element_typ...  27.5 us
    reshape x1, local copies, waits for them, and re-layouts, per_device(): outbound = outbound.reshape(slot_count, owner_count * row_count, full_width)  11.6 us
    convert_element_type x1, local copies, waits for them, and re-layouts, per_device(): scaled = (product * graft[:, None, None]).astype(jnp.bfloat16)  11.4 us
  transfers between devices with their start and end apart: 3, of which 2 were waited for; matrix products, arithmetic and copies ran while one was open for 1% of the time, Pallas kernels for 0%

commit v1 on v0

--- a/solution.py
+++ b/solution.py
@@ -1,10 +1,446 @@
+import functools
+
 import jax
 import jax.numpy as jnp
 from jax import lax
+from jax.experimental import pallas as pl
+from jax.experimental.pallas import tpu as pltpu
 from jax.sharding import PartitionSpec as P
 
-
-def per_device(grad_partial, second_moment, left_factor, right_factor, block_owner, block_slot):
+MESH = pl.DeviceIdType.MESH
+REPS = 4
+CHIPS = 16
+SIDE = 4
+PER_PLANE = 8
+HALF = PER_PLANE // 2
+ORDER_AT = 0
+DEST_AT = 32
+SLOT_AT = 96
+CORE_AT = 97
+PLACE_AT = 128
+FROM_AT = 160
+TABLE = 192
+
+
+def step_kernel(
+    tab, g_hbm, sm_hbm, l_hbm, r_hbm, upd_hbm, nm_hbm,
+    grad, sm, left, right, xs, a_in, b_in, c_in, c_out, summed, f_out, g_in,
+    lp, prod, pb0, pb1, pb2, pb3, ret, back, mom_in, nm, upd,
+    ad_x, ad_1, ad_p, ad_2, ad_3, rms,
+    sem_in, sem_out, x_send, x_recv, f_send, f_recv, d_send, d_recv,
+    p_send, p_recv, u_send, u_recv, m_send, m_recv, s_send, s_recv,
+):
+    pbs = (pb0, pb1, pb2, pb3)
+    f = lax.axis_index("fsdp")
+    x = lax.axis_index("rep")
+    core = f % 2
+    chip = f // 2
+    cy = chip // SIDE
+    cz = chip % SIDE
+    sibling = f + 1 - 2 * core
+    nblk, rows, width = grad.shape
+    quarter = width // REPS
+
+    def chip_at(i):
+        return ((cy + i // SIDE) % SIDE) * SIDE + (cz + i % SIDE) % SIDE
+
+    loads = [
+        pltpu.make_async_copy(src, dst, sem_in.at[i])
+        for i, (src, dst) in enumerate(
+            ((g_hbm, grad), (l_hbm, left), (r_hbm, right), (sm_hbm, sm))
+        )
+    ]
+    for load in loads:
+        load.start()
+
+    barrier = pltpu.get_barrier_semaphore()
+
+    def greet(i, _):
+        to = (chip_at(i // REPS) * 2 + core, (x + i % REPS) % REPS)
+        pl.semaphore_signal(barrier, inc=1, device_id=to, device_id_type=MESH)
+        return 0
+
+    lax.fori_loop(1, CHIPS * REPS, greet, 0)
+    pl.semaphore_signal(barrier, inc=1, device_id=(sibling, x), device_id_type=MESH)
+
+    slot = tab[SLOT_AT]
+    holder = tab[CORE_AT]
+    x_right, x_left, x_far = (x + 1) % REPS, (x + 3) % REPS, (x + 2) % REPS
+
+    def stage(k):
+        def body(t, _):
+            xs[k, t] = grad[tab[ORDER_AT + t], :, k * quarter : (k + 1) * quarter]
+            return 0
+
+        lax.fori_loop(0, nblk, body, 0, unroll=4)
+
+    def x_copy(k, n, src, dst, to):
+        i = k * 6 + n
+        return pltpu.make_async_remote_copy(
+            src, dst, x_send.at[i], x_recv.at[i], device_id=(f, to), device_id_type=MESH
+        )
+
+    def x_copies(k):
+        far, near_r, near_l = x_far * PER_PLANE, x_right * PER_PLANE, x_left * PER_PLANE
+        return (
+            x_copy(k, 0, xs.at[k, pl.ds(far, HALF)], a_in.at[0, k], x_right),
+            x_copy(k, 1, xs.at[k, pl.ds(far + HALF, HALF)], a_in.at[1, k], x_left),
+            x_copy(k, 2, xs.at[k, pl.ds(near_r + HALF, HALF)], b_in.at[0, k], x_right),
+            x_copy(k, 3, xs.at[k, pl.ds(near_l, HALF)], b_in.at[1, k], x_left),
+            x_copy(k, 4, c_out.at[0, k], c_in.at[0, k], x_right),
+            x_copy(k, 5, c_out.at[1, k], c_in.at[1, k], x_left),
+        )
+
+    xc = [x_copies(k) for k in range(REPS)]
+
+    def first(k):
+        for n in range(4):
+            xc[k][n].start()
+
+    def wide(v):
+        return v.astype(jnp.float32)
+
+    def merge(k):
+        for side, at in ((0, x_right * PER_PLANE), (1, x_left * PER_PLANE + HALF)):
+            xc[k][side].wait_recv()
+
+            def body(j, _):
+                c_out[side, k, j] = (wide(xs[k, at + j]) + wide(a_in[side, k, j])).astype(jnp.bfloat16)
+                return 0
+
+            lax.fori_loop(0, HALF, body, 0, unroll=True)
+            xc[k][4 + side].start()
+
+    def finish(k):
+        for n in (2, 3, 4, 5):
+            xc[k][n].wait_recv()
+        for lo, from_l, from_r in ((0, c_in, b_in), (HALF, b_in, c_in)):
+
+            def body(j, _):
+                total = wide(xs[k, x * PER_PLANE + lo + j]) + wide(from_l[0, k, j]) + wide(from_r[1, k, j])
+                summed[k, lo + j] = total.astype(jnp.bfloat16)
+                return 0
+
+            lax.fori_loop(0, HALF, body, 0, unroll=True)
+
+    def forward(k):
+        def body(i, _):
+            to = chip_at(i)
+            f_out[k, to] = summed[k, tab[DEST_AT + x * CHIPS + to]]
+            pltpu.make_async_remote_copy(
+                f_out.at[k, to], g_in.at[k, chip, core], f_send.at[k], f_recv.at[k],
+                device_id=(to * 2 + core, x), device_id_type=MESH,
+            ).start()
+            return 0
+
+        lax.fori_loop(1, CHIPS, body, 0)
+        g_in[k, chip, core] = summed[k, tab[DEST_AT + x * CHIPS + chip]]
+
+    def many(ref, send, recv):
+        return pltpu.make_async_remote_copy(
+            ref, ref, send, recv, device_id=(sibling, x), device_id_type=MESH
+        )
+
+    swaps = [
+        pltpu.make_async_remote_copy(
+            g_in.at[k, :, core], g_in.at[k, :, core], d_send.at[k], d_recv.at[k],
+            device_id=(sibling, x), device_id_type=MESH,
+        )
+        for k in range(REPS)
+    ]
+
+    def swap(k):
+        many(f_out.at[k, pl.ds(0, CHIPS - 1)], f_send.at[k], f_recv.at[k]).wait_recv()
+        swaps[k].start()
+
+    tile = width // 2
+
+    def left_mul(k):
+        swaps[k].wait_recv()
+
+        def body(i, _):
+            at = pl.multiple_of(i * tile, tile)
+            part = jnp.dot(
+                left[slot, pl.ds(at, tile), :], g_in[k].reshape(width, quarter),
+                preferred_element_type=jnp.float32,
+            )
+            lp[pl.ds(at, tile), k * quarter : (k + 1) * quarter] = part.astype(jnp.bfloat16)
+            return 0
+
+        lax.fori_loop(0, width // tile, body, 0)
+
+    loads[0].wait()
+    stage(0)
+    pl.semaphore_wait(barrier, CHIPS * REPS)
+    first(0)
+    stage(1)
+    first(1)
+    merge(0)
+    stage(2)
+    first(2)
+    merge(1)
+    finish(0)
+    forward(0)
+    stage(3)
+    first(3)
+    merge(2)
+    finish(1)
+    forward(1)
+    loads[1].wait()
+    swap(0)
+    merge(3)
+    left_mul(0)
+    finish(2)
+    forward(2)
+    swap(1)
+    left_mul(1)
+    finish(3)
+    forward(3)
+
+    moments = []
+    for i in range(1, REPS):
+        to = (x + i) % REPS
+        moments.append(
+            pltpu.make_async_remote_copy(
+                summed.at[to], mom_in.at[x], m_send.at[i], m_recv.at[i],
+                device_id=(f, to), device_id_type=MESH,
+            )
+        )
+        moments[-1].start()
+    mom_in[x] = summed[x]
+
+    swap(2)
+    left_mul(2)
+
+    loads[3].wait()
+    for copy in moments:
+        copy.wait_recv()
+
+    def moment(b, _):
+        t = tab[PLACE_AT + b]
+        s = wide(mom_in[t // PER_PLANE, t % PER_PLANE])
+        new = 0.99 * sm[b] + 0.01 * s * s
+        nm[b] = new
+        adam = s / (jnp.sqrt(new) + 1e-08)
+        sq = jnp.sum(adam * adam, axis=0, keepdims=True)
+        half = quarter // 2
+        ad_x[x, pl.ds(b, 1), :] = sq[:, :half] + sq[:, half:]
+        return 0
+
+    lax.fori_loop(0, nblk, moment, 0, unroll=2)
+    store_nm = pltpu.make_async_copy(nm, nm_hbm, sem_out.at[0])
+    store_nm.start()
+
+    sums_x = [
+        pltpu.make_async_remote_copy(
+            ad_x.at[x], ad_x.at[x], s_send.at[i], s_recv.at[i],
+            device_id=(f, (x + i) % REPS), device_id_type=MESH,
+        )
+        for i in range(1, REPS)
+    ]
+    for copy in sums_x:
+        copy.start()
+
+    swap(3)
+    left_mul(3)
+
+    for copy in sums_x:
+        copy.wait_recv()
+    ad_1[...] = (ad_x[0] + ad_x[1]) + (ad_x[2] + ad_x[3])
+
+    def sums_plane(i, _):
+        to = chip_at(i)
+        pltpu.make_async_remote_copy(
+            ad_1, ad_p.at[chip], s_send.at[0], s_recv.at[0],
+            device_id=(to * 2 + core, x), device_id_type=MESH,
+        ).start()
+        return 0
+
+    lax.fori_loop(1, CHIPS, sums_plane, 0)
+    ad_p[chip] = ad_1[...]
+
+    loads[2].wait()
+    squares = jnp.zeros((1, quarter), jnp.float32)
+    for i in range(REPS):
+        q = (x + i) % REPS
+        cols = pl.ds(pl.multiple_of(q * quarter, quarter), quarter)
+
+        def body(n, acc):
+            at = pl.multiple_of(n * tile, tile)
+            part = jnp.dot(
+                lp[pl.ds(at, tile), :], right[slot, :, cols], preferred_element_type=jnp.float32
+            )
+            prod[i, pl.ds(at, tile), :] = part
+            return acc + jnp.sum(part * part, axis=0, keepdims=True)
+
+        squares = lax.fori_loop(0, width // tile, body, squares)
+
+    many(ad_p.at[pl.ds(0, CHIPS - 1)], s_send.at[0], s_recv.at[0]).wait_recv()
+    ad_2[...] = jnp.sum(ad_p[...], axis=0)
+    sums_chip = pltpu.make_async_remote_copy(
+        ad_2, ad_3, s_send.at[REPS], s_recv.at[REPS], device_id=(sibling, x), device_id_type=MESH
+    )
+    sums_chip.start()
+
+    mean = jnp.sum(squares, axis=1, keepdims=True) / (width * width)
+    inverse = 1.0 / jnp.sqrt(mean + 1e-06)
+    trades = []
+    for i in range(REPS):
+        pb = pbs[i]
+
+        def body(n, _):
+            at = pl.multiple_of(n * 2 * rows, 2 * rows)
+            scaled = (prod[i, pl.ds(at, 2 * rows), :] * inverse).astype(jnp.bfloat16)
+            pb[core, n] = scaled.reshape(2, rows, quarter)
+            return 0
+
+        lax.fori_loop(0, CHIPS, body, 0, unroll=2)
+        trades.append(
+            pltpu.make_async_remote_copy(
+                pb.at[core, :, 1 - core], pb.at[core, :, 1 - core], p_send.at[i], p_recv.at[i],
+                device_id=(sibling, x), device_id_type=MESH,
+            )
+        )
+        trades[i].start()
+
+    for i in range(REPS):
+        pb = pbs[i]
+        q = (x + i) % REPS
+        trades[i].wait_recv()
+
+        def body(n, _):
+            to = chip_at(n)
+            ret[i, to] = pb[holder, to, core]
+            pltpu.make_async_remote_copy(
+                ret.at[i, to], back.at[x * CHIPS + chip], u_send.at[0], u_recv.at[0],
+                device_id=(to * 2 + core, q), device_id_type=MESH,
+            ).start()
+            return 0
+
+        lax.fori_loop(1 if i == 0 else 0, CHIPS, body, 0)
+        if i == 0:
+            back[x * CHIPS + chip] = pb[holder, chip, core]
+
+    sums_chip.wait_recv()
+    total = jnp.sum(ad_2[...] + ad_3[...], axis=1, keepdims=True)
+    rms[...] = jnp.broadcast_to(jnp.sqrt(total / (width * width)), rms.shape)
+
+    many(back.at[pl.ds(0, CHIPS * REPS - 1)], u_send.at[0], u_recv.at[0]).wait_recv()
+
+    def collect(b, _):
+        scale = rms[pl.ds(b, 1), :]
+        scale = jnp.concatenate([scale, scale], axis=1)
+        upd[b] = (wide(back[tab[FROM_AT + b]]) * scale).astype(jnp.bfloat16)
+        return 0
+
+    lax.fori_loop(0, nblk, collect, 0, unroll=2)
+    store_upd = pltpu.make_async_copy(upd, upd_hbm, sem_out.at[1])
+    store_upd.start()
+
+    for k in range(REPS):
+        for copy in xc[k]:
+            copy.wait_send()
+        many(f_out.at[k, pl.ds(0, CHIPS - 1)], f_send.at[k], f_recv.at[k]).wait_send()
+        swaps[k].wait_send()
+        trades[k].wait_send()
+    for copy in moments + sums_x + [sums_chip]:
+        copy.wait_send()
+    many(ad_p.at[pl.ds(0, CHIPS - 1)], s_send.at[0], s_recv.at[0]).wait_send()
+    many(back.at[pl.ds(0, CHIPS * REPS - 1)], u_send.at[0], u_recv.at[0]).wait_send()
+    store_nm.wait()
+    store_upd.wait()
+
+
+def one_kernel(grad, second_moment, left_factor, right_factor, table):
+    nblk, rows, width = grad.shape
+    slots = left_factor.shape[0]
+    quarter = width // REPS
+    bf, f32 = jnp.bfloat16, jnp.float32
+    piece = (rows, quarter)
+    any_spec = pl.BlockSpec(memory_space=pl.ANY)
+    vmem = pltpu.VMEM
+    dma = pltpu.SemaphoreType.DMA
+    return pl.pallas_call(
+        step_kernel,
+        out_shape=(
+            jax.ShapeDtypeStruct((nblk, rows, quarter), bf),
+            jax.ShapeDtypeStruct((nblk, rows, quarter), f32),
+        ),
+        in_specs=[pl.BlockSpec(memory_space=pltpu.SMEM)] + [any_spec] * 4,
+        out_specs=(any_spec, any_spec),
+        scratch_shapes=[
+            vmem((nblk, rows, width), bf),
+            vmem((nblk, rows, quarter), f32),
+            vmem((slots, width, width), bf),
+            vmem((slots, width, width), bf),
+            vmem((REPS, nblk) + piece, bf),
+            vmem((2, REPS, HALF) + piece, bf),
+            vmem((2, REPS, HALF) + piece, bf),
+            vmem((2, REPS, HALF) + piece, bf),
+            vmem((2, REPS, HALF) + piece, bf),
+            vmem((REPS, PER_PLANE) + piece, bf),
+            vmem((REPS, CHIPS) + piece, bf),
+            vmem((REPS, CHIPS, 2) + piece, bf),
+            vmem((width, width), bf),
+            vmem((REPS, width, quarter), f32),
+        ]
+        + [vmem((2, CHIPS, 2) + piece, bf)] * REPS
+        + [
+            vmem((REPS, CHIPS) + piece, bf),
+            vmem((REPS * CHIPS,) + piece, bf),
+            vmem((REPS, PER_PLANE) + piece, bf),
+            vmem((nblk,) + piece, f32),
+            vmem((nblk,) + piece, bf),
+            vmem((REPS, nblk, 128), f32),
+            vmem((nblk, 128), f32),
+            vmem((CHIPS, nblk, 128), f32),
+            vmem((nblk, 128), f32),
+            vmem((nblk, 128), f32),
+            vmem((nblk, 128), f32),
+            dma((4,)),
+            dma((2,)),
+            dma((REPS * 6,)),
+            dma((REPS * 6,)),
+        ]
+        + [dma((REPS,))] * 6
+        + [dma((1,)), dma((1,)), dma((REPS,)), dma((REPS,)), dma((REPS + 1,)), dma((REPS + 1,))],
+        compiler_params=pltpu.CompilerParams(
+            collective_id=0, has_side_effects=True, vmem_limit_bytes=58 << 20
+        ),
+        cost_estimate=pl.CostEstimate(
+            flops=4 * width**3, bytes_accessed=18 << 20, transcendentals=nblk * rows * quarter
+        ),
+        name="shampoo_step",
+    )(table, grad, second_moment, left_factor, right_factor)
+
+
+def tables(block_owner, block_slot):
+    f = lax.axis_index("fsdp")
+    x = lax.axis_index("rep")
+    nblk = block_owner.shape[0]
+    blocks = jnp.arange(nblk, dtype=jnp.int32)
+
+    def pick(values, hit):
+        return jnp.sum(jnp.where(hit, values, 0), axis=-1).astype(jnp.int32)
+
+    before = jnp.sum((block_owner[None, :] < block_owner[:, None]).astype(jnp.int32), axis=1)
+    place = before + block_slot
+    plane = place % REPS
+    within = place // REPS
+    sorted_at = plane * PER_PLANE + within
+    came_from = plane * CHIPS + block_owner // 2
+    sites = jnp.arange(REPS * CHIPS, dtype=jnp.int32)
+    order = pick(blocks[None, :], sorted_at[None, :] == blocks[:, None])
+    dest = pick(within[None, :], came_from[None, :] == sites[:, None])
+    slot = pick(block_slot, (block_owner == f) & (plane == x))
+    core = pick(block_owner % 2, came_from == x * CHIPS + f // 2)
+    pad = jnp.zeros((PLACE_AT - CORE_AT - 1,), jnp.int32)
+    table = jnp.concatenate([order, dest, slot[None], core[None], pad, sorted_at, came_from])
+    most = jnp.max(jnp.sum(((block_owner // 2)[None, :] == sites[:CHIPS, None]).astype(jnp.int32), axis=1))
+    return table, most
+
+
+def general(grad_partial, second_moment, left_factor, right_factor, block_owner, block_slot):
     slot_count = left_factor.shape[0]
     row_count = grad_partial.shape[2]
     full_width = grad_partial.shape[3]
@@ -22,8 +458,7 @@
     owned = (
         (block_slot[None, :] == slot_range[:, None]) & (block_owner[None, :] == owner_index)
     ).astype(jnp.float32)
-    local_grad = grad_partial[0].astype(jnp.float32)
-    summed = lax.psum(local_grad.astype(jnp.bfloat16), "rep").astype(jnp.float32)
+    summed = lax.psum(grad_partial[0], "rep").astype(jnp.float32)
     column = lax.dynamic_slice_in_dim(summed, rep_index * quarter, quarter, 2)
     new_moment = 0.99 * second_moment + 0.01 * column * column
     adam = column / (jnp.sqrt(new_moment) + 1e-08)
@@ -55,6 +490,21 @@
     return (update, new_moment)
 
 
+def per_device(grad_partial, second_moment, left_factor, right_factor, block_owner, block_slot):
+    table, most = tables(block_owner, block_slot)
+
+    def direct(gp, sm, lf, rf, _owner, _slot, tab):
+        return one_kernel(gp[0], sm, lf, rf, tab)
+
+    def fallback(gp, sm, lf, rf, owner, slot, _tab):
+        return general(gp, sm, lf, rf, owner, slot)
+
+    return lax.cond(
+        most <= REPS, direct, fallback,
+        grad_partial, second_moment, left_factor, right_factor, block_owner, block_slot, table,
+    )
+
+
 def solution(mesh):
     placed = (
         P("rep", None, "fsdp", None),

time: 468 us -> 95.1 us (0.20)
  the two profiles are of different devices: /device:TPU:48 before, /device:TPU:1 now
where the time goes in v1:
time: 95.1 us; the launch traced here: 95 us
  Pallas kernels  72.9 us (77%)
  between operations  14.7 us (15%)
  other arithmetic  4.01 us (4%)
  local copies, waits for them, and re-layouts  3.14 us (3%)
    pallas_call x1, Pallas kernels, one_kernel(): pl.pallas_call(step_kernel, out_shape=(jax.ShapeDtypeStruct((nblk, rows,...  72.9 us

profile of v1, /device:TPU:1, one launch (start us, length us, event | category | flops | bytes accessed | tf_op | source)
XLA Modules:
  0.0 95.0 jit_solution(13208277178999695824)
XLA Ops:
  7.2 0.9 convert_reduce_fusion
  8.1 1.3 %fusion.24 = (s32[]{:T(128)}, s32[]{:T(128)}, s32[32]{0:T(128)S(1)}, s32[32]{0:T(128)S(1)}, s32[32]{0:T(128)S(1)}) fusion(s32[]{:T(128)S(6)} %add.50, s32[32]{0:T(128)} %param.12, s32[32]{0:T(128)} %param.13, s32[]{:T(128)S(6)} %axis_index.45, s32[]{:T(128)S(6)} %axis_index.43, s32[32]{0:T(128)S(1)} %convert_reduce_fusion), kind=kLoop, calls=%fused_computation.52 | loop fusion | flops 1310 | bytes 788 | tf_op jit(solution)/shard_map/reduce_sum | solution.py:424
  9.4 0.2 convert_reduce_fusion.1
  9.6 0.7 reduce_max.9
  11.0 0.7 multiply_add_fusion.1
  11.7 0.1 select_reduce_fusion.1
  11.8 0.1 select_reduce_fusion.2
  11.9 1.4 %concatenate.3 = s32[192]{0:T(256)S(1)} concatenate(s32[32]{0:T(128)S(1)} %select_reduce_fusion.2, s32[64]{0:T(128)S(1)} %select_reduce_fusion.1, s32[1]{0:T(128)} %bitcast.9, s32[1]{0:T(128)} %bitcast.10, s32[30]{0:T(128)S(1)} %broadcast.97, s32[32]{0:T(128)S(1)} %get-tuple-element.87, s32[32]{0:T(128)S(1)} %get-tuple-element.84), dimensions={0} | concatenate | bytes 1536 | tf_op jit(solution)/shard_map/concatenate | solution.py:438
  13.3 73.1 %conditional.1 = (f32[32,32,256]{2,1,0:T(8,128)S(1)}, bf16[32,32,256]{2,1,0:T(8,128)(2,1)S(1)}) conditional(s32[]{:T(128)} %convert_element_type.29, (s32[32]{0:T(128)}, s32[32]{0:T(128)}, bf16[1,32,32,1024]{3,2,1,0:T(8,128)(2,1)}, bf16[3,1024,1024]{2,1,0:T(8,128)(2,1)}, bf16[3,1024,1024]{2,1,0:T(8,128)(2,1)}, ...), branch_computations={%region_7.13_spmd, %region_13.14_spmd} | conditional | flops 13159111680 | bytes 177739760 | solution.py:502
  13.5 72.9 %shampoo_step.1 = (bf16[32,32,256]{2,1,0:T(8,128)(2,1)S(1)}, f32[32,32,256]{2,1,0:T(8,128)S(1)}) custom-call(s32[192]{0:T(256)S(1)} %get-tuple-element.28.tab, bf16[32,32,1024]{2,1,0:T(8,128)(2,1)} %bitcast.29, f32[32,32,256]{2,1,0:T(8,128)} %get-tuple-element.30.sm_hbm, bf16[3,1024,1024]{2,1,0:T(8,128)(2,1)} %get-tuple-element.31.l_hbm, ...), custom_call_target="tpu_custom_call" | custom-call | flops 4294967296 | bytes 18874368 | tf_op jit(solution)/shard_map/cond/branch_1_fun/shampoo_step/pallas_call | solution.py:363
  86.4 0.8 copy.91
  87.1 1.0 %copy.92 = f32[32,32,256]{2,1,0:T(8,128)} copy(f32[32,32,256]{2,1,0:T(8,128)S(1)} %get-tuple-element.98) | data formatting | bytes 2097152
  (2 shorter events, 0.0 us)

commit v2 on v1

v2 whole, which is shorter than its diff:
```python
import functools

import jax
import jax.numpy as jnp
from jax import lax
from jax.experimental import pallas as pl
from jax.experimental.pallas import tpu as pltpu
from jax.sharding import PartitionSpec as P

MESH = pl.DeviceIdType.MESH
REPS = 4
CHIPS = 16
SIDE = 4
PER_PLANE = 8
HALF = PER_PLANE // 2


def step_kernel(
    owner, owner_slot, g_hbm, sm_hbm, l_hbm, r_hbm, upd_hbm, nm_hbm,
    grad, sm, left, right, xs, a_in, b_in, c_in, c_out, summed, f_out, g_in,
    lp, pb0, pb1, pb2, pb3, ret, back, mom_in, nm, upd,
    ad_1, ad_2, factor, place_v, place, inverse_v, inverse,
    sem_in, sem_out, x_send, x_recv, f_send, f_recv, d_send, d_recv,
    p_send, p_recv, u_send, u_recv, m_send, m_recv, s_send, s_recv,
):
    pbs = (pb0, pb1, pb2, pb3)
    f = lax.axis_index("fsdp")
    x = lax.axis_index("rep")
    core = f % 2
    chip = f // 2
    cy = chip // SIDE
    cz = chip % SIDE
    sibling = f + 1 - 2 * core
    nblk, rows, width = grad.shape
    quarter = width // REPS

    chips = [
        lax.rem(cy + i // SIDE, SIDE) * SIDE + lax.rem(cz + i % SIDE, SIDE) for i in range(CHIPS)
    ]
    reps = [lax.rem(x + i, REPS) for i in range(REPS)]

    loads = [
        pltpu.make_async_copy(src, dst, sem_in.at[i])
        for i, (src, dst) in enumerate(
            ((g_hbm, grad), (l_hbm, left), (r_hbm, right), (sm_hbm, sm))
        )
    ]
    for load in loads:
        load.start()

    barrier = pltpu.get_barrier_semaphore()

    for i in range(1, CHIPS * REPS):
        to = (chips[i // REPS] * 2 + core, reps[i % REPS])
        pl.semaphore_signal(barrier, inc=1, device_id=to, device_id_type=MESH)
    pl.semaphore_signal(barrier, inc=1, device_id=(sibling, x), device_id_type=MESH)

    lane = lax.broadcasted_iota(jnp.int32, place_v.shape, 1)
    line = lax.broadcasted_iota(jnp.int32, place_v.shape, 0)
    zero = jnp.zeros(place_v.shape, jnp.int32)
    owners, slots, before = zero, zero, zero
    for b in range(nblk):
        owners = jnp.where(lane == b, owner[b], owners)
        slots = jnp.where(lane == b, owner_slot[b], slots)
    for b in range(nblk):
        before = before + jnp.where(owners > owner[b], 1, 0)
    spot = before + slots
    plane_v = spot & (REPS - 1)
    sorted_v = plane_v * PER_PLANE + (spot >> 2)
    place_v[...] = jnp.where(line == 0, sorted_v, plane_v * CHIPS + (owners >> 1))
    to_scalar = pltpu.make_async_copy(place_v, place, sem_in.at[4])
    to_scalar.start()
    to_scalar.wait()
    order_v, dest_v = zero, zero
    slot = holder = mine = have = jnp.int32(0)
    for b in range(nblk):
        at, site = place[0, b], place[1, b]
        order_v = jnp.where(lane == at, b, order_v)
        dest_v = jnp.where(lane == site, at & (PER_PLANE - 1), dest_v)
        here = site == x * CHIPS + chip
        own = here & (owner[b] == f)
        holder = jnp.where(here, owner[b] & 1, holder)
        slot = jnp.where(own, owner_slot[b], slot)
        mine = jnp.where(own, b, mine)
        have = jnp.where(own, 1, have)
    inverse_v[...] = jnp.where(line == 0, order_v, dest_v)
    to_scalar = pltpu.make_async_copy(inverse_v, inverse, sem_in.at[5])
    to_scalar.start()
    to_scalar.wait()
    _, x_right, x_far, x_left = reps

    def stage(k):
        def body(t, _):
            xs[k, t] = grad[inverse[0, t], :, k * quarter : (k + 1) * quarter]
            return 0

        lax.fori_loop(0, nblk, body, 0, unroll=4)

    def x_copy(k, n, src, dst, to):
        i = k * 6 + n
        return pltpu.make_async_remote_copy(
            src, dst, x_send.at[i], x_recv.at[i], device_id=(f, to), device_id_type=MESH
        )

    def x_copies(k):
        far, near_r, near_l = x_far * PER_PLANE, x_right * PER_PLANE, x_left * PER_PLANE
        return (
            x_copy(k, 0, xs.at[k, pl.ds(far, HALF)], a_in.at[0, k], x_right),
            x_copy(k, 1, xs.at[k, pl.ds(far + HALF, HALF)], a_in.at[1, k], x_left),
            x_copy(k, 2, xs.at[k, pl.ds(near_r + HALF, HALF)], b_in.at[0, k], x_right),
            x_copy(k, 3, xs.at[k, pl.ds(near_l, HALF)], b_in.at[1, k], x_left),
            x_copy(k, 4, c_out.at[0, k], c_in.at[0, k], x_right),
            x_copy(k, 5, c_out.at[1, k], c_in.at[1, k], x_left),
        )

    xc = [x_copies(k) for k in range(REPS)]

    def first(k):
        xc[k][0].start()
        xc[k][1].start()

    def second(k):
        xc[k][2].start()
        xc[k][3].start()

    def wide(v):
        return v.astype(jnp.float32)

    def merge(k):
        for side, at in ((0, x_right * PER_PLANE), (1, x_left * PER_PLANE + HALF)):
            xc[k][side].wait_recv()

            def body(j, _):
                c_out[side, k, j] = (wide(xs[k, at + j]) + wide(a_in[side, k, j])).astype(jnp.bfloat16)
                return 0

            lax.fori_loop(0, HALF, body, 0, unroll=True)
            xc[k][4 + side].start()

    def finish(k):
        for n in (2, 3, 4, 5):
            xc[k][n].wait_recv()
        for lo, from_l, from_r in ((0, c_in, b_in), (HALF, b_in, c_in)):

            def body(j, _):
                total = wide(xs[k, x * PER_PLANE + lo + j]) + wide(from_l[0, k, j]) + wide(from_r[1, k, j])
                summed[k, lo + j] = total.astype(jnp.bfloat16)
                return 0

            lax.fori_loop(0, HALF, body, 0, unroll=True)

    def forward(k):
        for to in chips[1:]:
            f_out[k, to] = summed[k, inverse[1, x * CHIPS + to]]
            pltpu.make_async_remote_copy(
                f_out.at[k, to], g_in.at[k, chip, core], f_send.at[k], f_recv.at[k],
                device_id=(to * 2 + core, x), device_id_type=MESH,
            ).start()
        g_in[k, chip, core] = summed[k, inverse[1, x * CHIPS + chip]]

    def many(ref, send, recv):
        return pltpu.make_async_remote_copy(
            ref, ref, send, recv, device_id=(sibling, x), device_id_type=MESH
        )

    swaps = [
        pltpu.make_async_remote_copy(
            g_in.at[k, :, core], g_in.at[k, :, core], d_send.at[k], d_recv.at[k],
            device_id=(sibling, x), device_id_type=MESH,
        )
        for k in range(REPS)
    ]

    def swap(k):
        many(f_out.at[k, pl.ds(0, CHIPS - 1)], f_send.at[k], f_recv.at[k]).wait_recv()
        swaps[k].start()

    tile = width // 2

    def left_mul(k):
        swaps[k].wait_recv()

        def body(i, _):
            at = pl.multiple_of(i * tile, tile)
            part = jnp.dot(
                left[slot, pl.ds(at, tile), :], g_in[k].reshape(width, quarter),
                preferred_element_type=jnp.float32,
            )
            lp[pl.ds(at, tile), k * quarter : (k + 1) * quarter] = part.astype(jnp.bfloat16)
            return 0

        lax.fori_loop(0, width // tile, body, 0)

    loads[0].wait()
    stage(0)
    pl.semaphore_wait(barrier, CHIPS * REPS)
    first(0)
    second(0)
    stage(1)
    first(1)
    merge(0)
    second(1)
    stage(2)
    first(2)
    merge(1)
    second(2)
    finish(0)
    forward(0)
    stage(3)
    first(3)
    merge(2)
    second(3)
    finish(1)
    forward(1)
    loads[1].wait()
    swap(0)
    merge(3)
    left_mul(0)
    finish(2)
    forward(2)
    swap(1)
    left_mul(1)
    finish(3)
    forward(3)

    moments = []
    for i in range(1, REPS):
        to = reps[i]
        moments.append(
            pltpu.make_async_remote_copy(
                summed.at[to], mom_in.at[x], m_send.at[i], m_recv.at[i],
                device_id=(f, to), device_id_type=MESH,
            )
        )
        moments[-1].start()
    mom_in[x] = summed[x]

    swap(2)
    left_mul(2)

    loads[2].wait()
    swap(3)
    left_mul(3)

    halves = width // tile
    chips_per = CHIPS // halves

    def right_mul(i, squares):
        cols = pl.ds(pl.multiple_of(reps[i] * quarter, quarter), quarter)

        def body(n, acc):
            at = pl.multiple_of(n * tile, tile)
            part = jnp.dot(
                lp[pl.ds(at, tile), :], right[slot, :, cols], preferred_element_type=jnp.float32
            )
            pbs[i][core, pl.ds(n * chips_per, chips_per)] = part.astype(jnp.bfloat16).reshape(
                chips_per, 2, rows, quarter
            )
            return acc + jnp.sum(part * part, axis=0, keepdims=True)

        return lax.fori_loop(0, halves, body, squares)

    trades = [
        pltpu.make_async_remote_copy(
            pb.at[core, :, 1 - core], pb.at[core, :, 1 - core], p_send.at[i], p_recv.at[i],
            device_id=(sibling, x), device_id_type=MESH,
        )
        for i, pb in enumerate(pbs)
    ]

    def send_back(i):
        pb = pbs[i]
        trades[i].wait_recv()
        for to in chips[1:] if i == 0 else chips:
            ret[i, to] = pb[holder, to, core]
            pltpu.make_async_remote_copy(
                ret.at[i, to], back.at[x * CHIPS + chip], u_send.at[0], u_recv.at[0],
                device_id=(to * 2 + core, reps[i]), device_id_type=MESH,
            ).start()
        if i == 0:
            back[x * CHIPS + chip] = pb[holder, chip, core]

    squares = jnp.zeros((1, quarter), jnp.float32)
    for i in range(REPS):
        squares = right_mul(i, squares)
        trades[i].start()
        if i in (1, 2):
            send_back(i - 1)

    loads[3].wait()
    for copy in moments:
        copy.wait_recv()

    at_lane = lax.broadcasted_iota(jnp.int32, (1, 128), 1)

    def moment(b, sums):
        t = place[0, b]
        s = wide(mom_in[t >> 3, t & (PER_PLANE - 1)])
        new = 0.99 * sm[b] + 0.01 * s * s
        nm[b] = new
        adam = s / (jnp.sqrt(new) + 1e-08)
        sq = jnp.sum(adam * adam, axis=0, keepdims=True)
        return jnp.where(at_lane == b, jnp.sum(sq, axis=1, keepdims=True), sums)

    owned = (at_lane == nblk + mine) & (have == 1)
    own_sums = jnp.where(owned, jnp.sum(squares, axis=1, keepdims=True), 0.0)
    own_sums = lax.fori_loop(0, nblk, moment, own_sums, unroll=4)
    ad_1[pl.ds(0, 1), :] = own_sums
    sums_chip = pltpu.make_async_remote_copy(
        ad_1.at[pl.ds(0, 1)], ad_1.at[pl.ds(8, 1)], s_send.at[0], s_recv.at[0],
        device_id=(sibling, x), device_id_type=MESH,
    )
    sums_chip.start()
    store_nm = pltpu.make_async_copy(nm, nm_hbm, sem_out.at[0])
    store_nm.start()
    sums_chip.wait_recv()
    ad_2[x * CHIPS + chip] = jnp.broadcast_to(own_sums + ad_1[pl.ds(8, 1), :], ad_2.shape[1:])
    for i in range(1, CHIPS * REPS):
        pltpu.make_async_remote_copy(
            ad_2.at[x * CHIPS + chip], ad_2.at[x * CHIPS + chip], s_send.at[1], s_recv.at[1],
            device_id=(chips[i // REPS] * 2 + core, reps[i % REPS]), device_id_type=MESH,
        ).start()
    send_back(2)
    send_back(3)

    many(ad_2.at[pl.ds(0, CHIPS * REPS - 1)], s_send.at[1], s_recv.at[1]).wait_recv()
    total = jnp.sum(ad_2[...], axis=0)
    line = lax.broadcasted_iota(jnp.int32, (nblk, 128), 0)
    lane = lax.broadcasted_iota(jnp.int32, (nblk, 128), 1)
    total = jnp.broadcast_to(total[:1, :], (nblk, 128))
    area = width * width
    adam_mean = jnp.sum(jnp.where(lane == line, total, 0.0), axis=1, keepdims=True) / area
    prod_mean = jnp.sum(jnp.where(lane == line + nblk, total, 0.0), axis=1, keepdims=True) / area
    scale = jnp.sqrt(adam_mean) / jnp.sqrt(prod_mean + 1e-06)
    factor[...] = jnp.broadcast_to(scale, factor.shape)

    many(back.at[pl.ds(0, CHIPS * REPS - 1)], u_send.at[0], u_recv.at[0]).wait_recv()

    def collect(b, _):
        by = factor[pl.ds(b, 1), :]
        by = jnp.concatenate([by, by], axis=1)
        upd[b] = (wide(back[place[1, b]]) * by).astype(jnp.bfloat16)
        return 0

    lax.fori_loop(0, nblk, collect, 0, unroll=2)
    store_upd = pltpu.make_async_copy(upd, upd_hbm, sem_out.at[1])
    store_upd.start()

    for k in range(REPS):
        for copy in xc[k]:
            copy.wait_send()
        many(f_out.at[k, pl.ds(0, CHIPS - 1)], f_send.at[k], f_recv.at[k]).wait_send()
        swaps[k].wait_send()
        trades[k].wait_send()
    for copy in moments + [sums_chip]:
        copy.wait_send()
    many(ad_2.at[pl.ds(0, CHIPS * REPS - 1)], s_send.at[1], s_recv.at[1]).wait_send()
    many(back.at[pl.ds(0, CHIPS * REPS - 1)], u_send.at[0], u_recv.at[0]).wait_send()
    store_nm.wait()
    store_upd.wait()


def one_kernel(grad, second_moment, left_factor, right_factor, block_owner, block_slot):
    nblk, rows, width = grad.shape
    slots = left_factor.shape[0]
    quarter = width // REPS
    bf, f32 = jnp.bfloat16, jnp.float32
    piece = (rows, quarter)
    any_spec = pl.BlockSpec(memory_space=pl.ANY)
    vmem = pltpu.VMEM
    dma = pltpu.SemaphoreType.DMA
    return pl.pallas_call(
        step_kernel,
        out_shape=(
            jax.ShapeDtypeStruct((nblk, rows, quarter), bf),
            jax.ShapeDtypeStruct((nblk, rows, quarter), f32),
        ),
        in_specs=[pl.BlockSpec(memory_space=pltpu.SMEM)] * 2 + [any_spec] * 4,
        out_specs=(any_spec, any_spec),
        scratch_shapes=[
            vmem((nblk, rows, width), bf),
            vmem((nblk, rows, quarter), f32),
            vmem((slots, width, width), bf),
            vmem((slots, width, width), bf),
            vmem((REPS, nblk) + piece, bf),
            vmem((2, REPS, HALF) + piece, bf),
            vmem((2, REPS, HALF) + piece, bf),
            vmem((2, REPS, HALF) + piece, bf),
            vmem((2, REPS, HALF) + piece, bf),
            vmem((REPS, PER_PLANE) + piece, bf),
            vmem((REPS, CHIPS) + piece, bf),
            vmem((REPS, CHIPS, 2) + piece, bf),
            vmem((width, width), bf),
        ]
        + [vmem((2, CHIPS, 2) + piece, bf)] * REPS
        + [
            vmem((REPS, CHIPS) + piece, bf),
            vmem((REPS * CHIPS,) + piece, bf),
            vmem((REPS, PER_PLANE) + piece, bf),
            vmem((nblk,) + piece, f32),
            vmem((nblk,) + piece, bf),
            vmem((16, 128), f32),
            vmem((REPS * CHIPS, 8, 128), f32),
            vmem((nblk, 128), f32),
            vmem((8, 128), jnp.int32),
            pltpu.SMEM((8, 128), jnp.int32),
            vmem((8, 128), jnp.int32),
            pltpu.SMEM((8, 128), jnp.int32),
            dma((6,)),
            dma((2,)),
            dma((REPS * 6,)),
            dma((REPS * 6,)),
        ]
        + [dma((REPS,))] * 6
        + [dma((1,)), dma((1,)), dma((REPS,)), dma((REPS,)), dma((2,)), dma((2,))],
        compiler_params=pltpu.CompilerParams(
            collective_id=0, has_side_effects=True, vmem_limit_bytes=58 << 20
        ),
        cost_estimate=pl.CostEstimate(
            flops=4 * width**3, bytes_accessed=18 << 20, transcendentals=nblk * rows * quarter
        ),
        name="shampoo_step",
    )(block_owner, block_slot, grad, second_moment, left_factor, right_factor)


def crowded(block_owner, block_slot):
    bit = jnp.left_shift(jnp.int32(1), block_owner)
    other = jnp.left_shift(jnp.int32(1), block_owner ^ 1)
    third = jnp.sum(jnp.where(block_slot == 2, bit, 0))
    second = jnp.sum(jnp.where(block_slot == 1, other, 0))
    return (third & second) != 0


def ring_sum(value, axis):
    count = lax.axis_size(axis)
    step = 1
    while step < count:
        value = value + lax.ppermute(value, axis, [(i, i ^ step) for i in range(count)])
        step *= 2
    return value


def general(grad_partial, second_moment, left_factor, right_factor, block_owner, block_slot):
    slot_count = left_factor.shape[0]
    row_count = grad_partial.shape[2]
    full_width = grad_partial.shape[3]
    rep_count = lax.axis_size("rep")
    owner_count = lax.axis_size("fsdp")
    owner_index = lax.axis_index("fsdp")
    rep_index = lax.axis_index("rep")
    quarter = full_width // rep_count
    slot_range = jnp.arange(slot_count, dtype=jnp.int32)
    owner_range = jnp.arange(owner_count, dtype=jnp.int32)
    selector = (
        (block_slot[None, None, :] == slot_range[:, None, None])
        & (block_owner[None, None, :] == owner_range[None, :, None])
    ).astype(jnp.bfloat16)
    owned = (
        (block_slot[None, :] == slot_range[:, None]) & (block_owner[None, :] == owner_index)
    ).astype(jnp.float32)
    summed = ring_sum(grad_partial[0].astype(jnp.float32), "rep")
    column = lax.dynamic_slice_in_dim(summed, rep_index * quarter, quarter, 2)
    new_moment = 0.99 * second_moment + 0.01 * column * column
    adam = column / (jnp.sqrt(new_moment) + 1e-08)
    partial_squares = jnp.sum(adam * adam, axis=(1, 2))
    total_squares = ring_sum(ring_sum(partial_squares, "rep"), "fsdp")
    adam_rms = jnp.sqrt(total_squares / (full_width * full_width))
    slot_rms = jnp.sum(owned * adam_rms[None, :], axis=1)
    grad_bf = summed.astype(jnp.bfloat16)
    outbound = jnp.einsum(
        "kdn,nrc->kdrc", selector, grad_bf, preferred_element_type=jnp.float32
    ).astype(jnp.bfloat16)
    outbound = outbound.reshape(slot_count, owner_count * row_count, full_width)
    inbound = lax.all_to_all(outbound, "fsdp", split_axis=1, concat_axis=1, tiled=True)
    left_prod = jnp.einsum(
        "kij,kjc->kic", left_factor, inbound, preferred_element_type=jnp.float32
    ).astype(jnp.bfloat16)
    product = jnp.einsum(
        "kij,kjc->kic", left_prod, right_factor, preferred_element_type=jnp.float32
    )
    prod_mean = jnp.mean(product * product, axis=(1, 2))
    graft = slot_rms / jnp.sqrt(prod_mean + 1e-06)
    scaled = (product * graft[:, None, None]).astype(jnp.bfloat16)
    returned = lax.all_to_all(scaled, "fsdp", split_axis=1, concat_axis=1, tiled=True)
    returned = lax.dynamic_slice_in_dim(returned, rep_index * quarter, quarter, 2)
    returned = returned.reshape(slot_count, owner_count, row_count, quarter)
    update = jnp.einsum(
        "kdn,kdrc->nrc", selector, returned, preferred_element_type=jnp.float32
    ).astype(jnp.bfloat16)
    return (update, new_moment)


def per_device(grad_partial, second_moment, left_factor, right_factor, block_owner, block_slot):
    def direct(gp, sm, lf, rf, owner, slot):
        return one_kernel(gp[0], sm, lf, rf, owner, slot)

    return lax.cond(
        crowded(block_owner, block_slot), general, direct,
        grad_partial, second_moment, left_factor, right_factor, block_owner, block_slot,
    )


def solution(mesh):
    placed = (
        P("rep", None, "fsdp", None),
        P(None, "fsdp", "rep"),
        P("fsdp", None, None),
        P("fsdp", None, None),
        P(),
        P(),
    )
    return jax.shard_map(
        per_device,
        mesh=mesh,
        in_specs=placed,
        out_specs=(P(None, "fsdp", "rep"), P(None, "fsdp", "rep")),
        check_vma=False,
    )
```

time: 95.1 us -> 70.2 us (0.74)
  between operations: 14.7 us -> 1.94 us
  Pallas kernels: 72.9 us -> 64.6 us
  other arithmetic: 4.01 us -> 1.32 us
  local copies, waits for them, and re-layouts: 3.14 us -> 1.77 us
    pallas_call x1, Pallas kernels: 72.9 us -> 64.6 us  [one_kernel(): pl.pallas_call(step_kernel, out_shape=(jax.ShapeDtypeStruct((nblk, rows,...]
    concatenate x1 -> x0, local copies, waits for them, and re-layouts: 1.38 us -> none  [tables(): jnp.concatenate([order, dest, slot[None], core[None], pad, sorted_at, cam...]
    reduce_sum x5 -> x1, other arithmetic: 2.62 us -> 1.32 us  [crowded(): second = jnp.sum(jnp.where(block_slot == 1, other, 0))]
where the time goes in v2:
time: 70.2 us; the launch traced here: 69.9 us
  Pallas kernels  64.6 us (92%)
  between operations  1.94 us (3%)
  local copies, waits for them, and re-layouts  1.77 us (3%)
  other arithmetic  1.32 us (2%)
    pallas_call x1, Pallas kernels, one_kernel(): pl.pallas_call(step_kernel, out_shape=(jax.ShapeDtypeStruct((nblk, rows,...  64.6 us
    unnamed x2, local copies, waits for them, and re-layouts  1.77 us

profile of v2, /device:TPU:1, one launch (start us, length us, event | category | flops | bytes accessed | tf_op | source)
XLA Modules:
  0.0 69.9 jit_solution(11649387796737505361)
XLA Ops:
  0.6 1.3 %fusion.25 = (s32[]{:T(128)}, s32[]{:T(128)}) fusion(s32[32]{0:T(128)} %param.13, s32[32]{0:T(128)} %param.12), kind=kLoop, calls=%fused_computation.35 | loop fusion | flops 286 | bytes 264 | tf_op jit(solution)/shard_map/reduce_sum | solution.py:430
  3.2 64.9 %conditional.1 = ((bf16[32,32,256]{2,1,0:T(8,128)(2,1)S(1)}, f32[32,32,256]{2,1,0:T(8,128)S(1)})) conditional(s32[]{:T(128)} %convert_element_type.27, (bf16[1,32,32,1024]{3,2,1,0:T(8,128)(2,1)}, s32[32]{0:T(128)}, s32[32]{0:T(128)}, f32[32,32,256]{2,1,0:T(8,128)}, bf16[3,1024,1024]{2,1,0:T(8,128)(2,1)}, ...), branch_computations={%region_2.3_spmd, %region_3.7_spmd} | conditional | flops 13163043840 | bytes 251670464 | solution.py:497
  3.3 64.6 %shampoo_step.1 = (bf16[32,32,256]{2,1,0:T(8,128)(2,1)S(1)}, f32[32,32,256]{2,1,0:T(8,128)S(1)}) custom-call(s32[32]{0:T(128)} %get-tuple-element.24.owner, s32[32]{0:T(128)} %get-tuple-element.25.owner_slot, bf16[32,32,1024]{2,1,0:T(8,128)(2,1)} %bitcast.27, f32[32,32,256]{2,1,0:T(8,128)} %get-tuple-element.27.sm_hbm, ...), custom_call_target="tpu_custom_call" | custom-call | flops 4294967296 | bytes 18874368 | tf_op jit(solution)/shard_map/cond/branch_0_fun/shampoo_step/pallas_call | solution.py:372
  68.1 0.8 %copy.79 = bf16[32,32,256]{2,1,0:T(8,128)(2,1)} copy(bf16[32,32,256]{2,1,0:T(8,128)(2,1)S(1)} %get-tuple-element.86) | data formatting | bytes 1048576
  68.9 1.0 %copy.80 = f32[32,32,256]{2,1,0:T(8,128)} copy(f32[32,32,256]{2,1,0:T(8,128)S(1)} %get-tuple-element.87) | data formatting | bytes 2097152

commit v3 on v2

--- a/solution.py
+++ b/solution.py
@@ -13,13 +13,14 @@
 SIDE = 4
 PER_PLANE = 8
 HALF = PER_PLANE // 2
+CUTS = 4
 
 
 def step_kernel(
     owner, owner_slot, g_hbm, sm_hbm, l_hbm, r_hbm, upd_hbm, nm_hbm,
     grad, sm, left, right, xs, a_in, b_in, c_in, c_out, summed, f_out, g_in,
     lp, pb0, pb1, pb2, pb3, ret, back, mom_in, nm, upd,
-    ad_1, ad_2, factor, place_v, place, inverse_v, inverse,
+    ad_1, ad_x, ad_p, factor, place_v, place, inverse_v, inverse,
     sem_in, sem_out, x_send, x_recv, f_send, f_recv, d_send, d_recv,
     p_send, p_recv, u_send, u_recv, m_send, m_recv, s_send, s_recv,
 ):
@@ -33,6 +34,8 @@
     sibling = f + 1 - 2 * core
     nblk, rows, width = grad.shape
     quarter = width // REPS
+    cut = width // CUTS
+    per_quarter = CUTS // REPS
 
     chips = [
         lax.rem(cy + i // SIDE, SIDE) * SIDE + lax.rem(cz + i % SIDE, SIDE) for i in range(CHIPS)
@@ -89,17 +92,21 @@
     to_scalar.wait()
     _, x_right, x_far, x_left = reps
 
+    def many(ref, send, recv):
+        return pltpu.make_async_remote_copy(
+            ref, ref, send, recv, device_id=(sibling, x), device_id_type=MESH
+        )
+
     def stage(k):
         def body(t, _):
-            xs[k, t] = grad[inverse[0, t], :, k * quarter : (k + 1) * quarter]
+            xs[k, t] = grad[inverse[0, t], :, k * cut : (k + 1) * cut]
             return 0
 
         lax.fori_loop(0, nblk, body, 0, unroll=4)
 
     def x_copy(k, n, src, dst, to):
-        i = k * 6 + n
         return pltpu.make_async_remote_copy(
-            src, dst, x_send.at[i], x_recv.at[i], device_id=(f, to), device_id_type=MESH
+            src, dst, x_send.at[0], x_recv.at[k, min(n // 2, 1)], device_id=(f, to), device_id_type=MESH
         )
 
     def x_copies(k):
@@ -113,7 +120,7 @@
             x_copy(k, 5, c_out.at[1, k], c_in.at[1, k], x_left),
         )
 
-    xc = [x_copies(k) for k in range(REPS)]
+    xc = [x_copies(k) for k in range(CUTS)]
 
     def first(k):
         xc[k][0].start()
@@ -127,8 +134,8 @@
         return v.astype(jnp.float32)
 
     def merge(k):
+        many(xs.at[k, pl.ds(0, PER_PLANE)], x_send.at[0], x_recv.at[k, 0]).wait_recv()
         for side, at in ((0, x_right * PER_PLANE), (1, x_left * PER_PLANE + HALF)):
-            xc[k][side].wait_recv()
 
             def body(j, _):
                 c_out[side, k, j] = (wide(xs[k, at + j]) + wide(a_in[side, k, j])).astype(jnp.bfloat16)
@@ -138,8 +145,7 @@
             xc[k][4 + side].start()
 
     def finish(k):
-        for n in (2, 3, 4, 5):
-            xc[k][n].wait_recv()
+        many(xs.at[k, pl.ds(0, 2 * PER_PLANE)], x_send.at[0], x_recv.at[k, 1]).wait_recv()
         for lo, from_l, from_r in ((0, c_in, b_in), (HALF, b_in, c_in)):
 
             def body(j, _):
@@ -153,153 +159,121 @@
         for to in chips[1:]:
             f_out[k, to] = summed[k, inverse[1, x * CHIPS + to]]
             pltpu.make_async_remote_copy(
-                f_out.at[k, to], g_in.at[k, chip, core], f_send.at[k], f_recv.at[k],
+                f_out.at[k, to], g_in.at[k, chip, core], f_send.at[0], f_recv.at[k],
                 device_id=(to * 2 + core, x), device_id_type=MESH,
             ).start()
         g_in[k, chip, core] = summed[k, inverse[1, x * CHIPS + chip]]
 
-    def many(ref, send, recv):
-        return pltpu.make_async_remote_copy(
-            ref, ref, send, recv, device_id=(sibling, x), device_id_type=MESH
-        )
-
     swaps = [
         pltpu.make_async_remote_copy(
-            g_in.at[k, :, core], g_in.at[k, :, core], d_send.at[k], d_recv.at[k],
+            g_in.at[k, :, core], g_in.at[k, :, core], d_send.at[0], d_recv.at[k],
             device_id=(sibling, x), device_id_type=MESH,
         )
-        for k in range(REPS)
+        for k in range(CUTS)
     ]
 
     def swap(k):
-        many(f_out.at[k, pl.ds(0, CHIPS - 1)], f_send.at[k], f_recv.at[k]).wait_recv()
+        many(f_out.at[k, pl.ds(0, CHIPS - 1)], f_send.at[0], f_recv.at[k]).wait_recv()
         swaps[k].start()
 
-    tile = width // 2
-
-    def left_mul(k):
-        swaps[k].wait_recv()
-
-        def body(i, _):
-            at = pl.multiple_of(i * tile, tile)
-            part = jnp.dot(
-                left[slot, pl.ds(at, tile), :], g_in[k].reshape(width, quarter),
-                preferred_element_type=jnp.float32,
-            )
-            lp[pl.ds(at, tile), k * quarter : (k + 1) * quarter] = part.astype(jnp.bfloat16)
-            return 0
-
-        lax.fori_loop(0, width // tile, body, 0)
+    def left_mul(m):
+        parts = range(m * per_quarter, (m + 1) * per_quarter)
+        for k in parts:
+            swaps[k].wait_recv()
+
+        block = jnp.concatenate([g_in[k].reshape(width, cut) for k in parts], axis=1)
+        part = jnp.dot(left[slot], block, preferred_element_type=jnp.float32)
+        lp[:, m * quarter : (m + 1) * quarter] = part.astype(jnp.bfloat16)
 
     loads[0].wait()
     stage(0)
     pl.semaphore_wait(barrier, CHIPS * REPS)
     first(0)
     second(0)
-    stage(1)
-    first(1)
-    merge(0)
-    second(1)
-    stage(2)
-    first(2)
-    merge(1)
-    second(2)
-    finish(0)
-    forward(0)
-    stage(3)
-    first(3)
-    merge(2)
-    second(3)
-    finish(1)
-    forward(1)
+    for k in range(1, CUTS + 1):
+        if k < CUTS:
+            stage(k)
+            first(k)
+        merge(k - 1)
+        if k < CUTS:
+            second(k)
+        if k == CUTS:
+            swap(0)
+        if k >= 2:
+            finish(k - 2)
+            forward(k - 2)
     loads[1].wait()
-    swap(0)
-    merge(3)
     left_mul(0)
-    finish(2)
-    forward(2)
     swap(1)
     left_mul(1)
-    finish(3)
-    forward(3)
-
-    moments = []
+    finish(CUTS - 1)
+    forward(CUTS - 1)
+
     for i in range(1, REPS):
         to = reps[i]
-        moments.append(
-            pltpu.make_async_remote_copy(
-                summed.at[to], mom_in.at[x], m_send.at[i], m_recv.at[i],
-                device_id=(f, to), device_id_type=MESH,
-            )
-        )
-        moments[-1].start()
-    mom_in[x] = summed[x]
+        pltpu.make_async_remote_copy(
+            summed.at[pl.ds(to * per_quarter, per_quarter)], mom_in.at[x], m_send.at[0], m_recv.at[0],
+            device_id=(f, to), device_id_type=MESH,
+        ).start()
+    mom_in[x] = summed[pl.ds(x * per_quarter, per_quarter)]
 
     swap(2)
     left_mul(2)
-
     loads[2].wait()
     swap(3)
     left_mul(3)
 
-    halves = width // tile
-    chips_per = CHIPS // halves
-
     def right_mul(i, squares):
         cols = pl.ds(pl.multiple_of(reps[i] * quarter, quarter), quarter)
-
-        def body(n, acc):
-            at = pl.multiple_of(n * tile, tile)
-            part = jnp.dot(
-                lp[pl.ds(at, tile), :], right[slot, :, cols], preferred_element_type=jnp.float32
-            )
-            pbs[i][core, pl.ds(n * chips_per, chips_per)] = part.astype(jnp.bfloat16).reshape(
-                chips_per, 2, rows, quarter
-            )
-            return acc + jnp.sum(part * part, axis=0, keepdims=True)
-
-        return lax.fori_loop(0, halves, body, squares)
+        part = jnp.dot(lp[...], right[slot, :, cols], preferred_element_type=jnp.float32)
+        pbs[i][core] = part.astype(jnp.bfloat16).reshape(CHIPS, 2, rows, quarter)
+        return squares + jnp.sum(part * part, axis=0, keepdims=True)
 
     trades = [
         pltpu.make_async_remote_copy(
-            pb.at[core, :, 1 - core], pb.at[core, :, 1 - core], p_send.at[i], p_recv.at[i],
+            pb.at[core, :, 1 - core], pb.at[core, :, 1 - core], p_send.at[0], p_recv.at[i],
             device_id=(sibling, x), device_id_type=MESH,
         )
         for i, pb in enumerate(pbs)
     ]
 
-    def send_back(i):
-        pb = pbs[i]
-        trades[i].wait_recv()
-        for to in chips[1:] if i == 0 else chips:
-            ret[i, to] = pb[holder, to, core]
-            pltpu.make_async_remote_copy(
-                ret.at[i, to], back.at[x * CHIPS + chip], u_send.at[0], u_recv.at[0],
-                device_id=(to * 2 + core, reps[i]), device_id_type=MESH,
-            ).start()
-        if i == 0:
-            back[x * CHIPS + chip] = pb[holder, chip, core]
+    def send_back(*which):
+        for i in which:
+            trades[i].wait_recv()
+        for to in chips:
+            for i in which:
+                if i == 0 and to is chips[0]:
+                    back[x * CHIPS + chip] = pbs[i][holder, chip, core]
+                    continue
+                ret[i, to] = pbs[i][holder, to, core]
+                pltpu.make_async_remote_copy(
+                    ret.at[i, to], back.at[x * CHIPS + chip], u_send.at[0], u_recv.at[0],
+                    device_id=(to * 2 + core, reps[i]), device_id_type=MESH,
+                ).start()
 
     squares = jnp.zeros((1, quarter), jnp.float32)
-    for i in range(REPS):
+    for i in (2, 0, 1, 3):
         squares = right_mul(i, squares)
         trades[i].start()
-        if i in (1, 2):
-            send_back(i - 1)
+        if i == 1:
+            send_back(2, 0)
 
     loads[3].wait()
-    for copy in moments:
-        copy.wait_recv()
+    moments = many(xs.at[0, pl.ds(0, (REPS - 1) * PER_PLANE)], m_send.at[0], m_recv.at[0])
+    moments.wait_recv()
 
     at_lane = lax.broadcasted_iota(jnp.int32, (1, 128), 1)
 
     def moment(b, sums):
         t = place[0, b]
-        s = wide(mom_in[t >> 3, t & (PER_PLANE - 1)])
-        new = 0.99 * sm[b] + 0.01 * s * s
-        nm[b] = new
-        adam = s / (jnp.sqrt(new) + 1e-08)
-        sq = jnp.sum(adam * adam, axis=0, keepdims=True)
+        sq = jnp.zeros((1, cut), jnp.float32)
+        for h in range(per_quarter):
+            s = wide(mom_in[t >> 3, h, t & (PER_PLANE - 1)])
+            at = slice(h * cut, (h + 1) * cut)
+            new = 0.99 * sm[b, :, at] + 0.01 * s * s
+            nm[b, :, at] = new
+            adam = s / (jnp.sqrt(new) + 1e-08)
+            sq = sq + jnp.sum(adam * adam, axis=0, keepdims=True)
         return jnp.where(at_lane == b, jnp.sum(sq, axis=1, keepdims=True), sums)
 
     owned = (at_lane == nblk + mine) & (have == 1)
@@ -314,20 +288,29 @@
     store_nm = pltpu.make_async_copy(nm, nm_hbm, sem_out.at[0])
     store_nm.start()
     sums_chip.wait_recv()
-    ad_2[x * CHIPS + chip] = jnp.broadcast_to(own_sums + ad_1[pl.ds(8, 1), :], ad_2.shape[1:])
-    for i in range(1, CHIPS * REPS):
+    ad_x[x, pl.ds(0, 1), :] = own_sums + ad_1[pl.ds(8, 1), :]
+    for i in range(1, REPS):
         pltpu.make_async_remote_copy(
-            ad_2.at[x * CHIPS + chip], ad_2.at[x * CHIPS + chip], s_send.at[1], s_recv.at[1],
-            device_id=(chips[i // REPS] * 2 + core, reps[i % REPS]), device_id_type=MESH,
+            ad_x.at[x, pl.ds(0, 1)], ad_x.at[x, pl.ds(0, 1)], s_send.at[1], s_recv.at[1],
+            device_id=(f, reps[i]), device_id_type=MESH,
         ).start()
-    send_back(2)
+    send_back(1)
+    sums_x = many(ad_x.at[pl.ds(0, REPS - 1), pl.ds(0, 1)], s_send.at[1], s_recv.at[1])
+    sums_x.wait_recv()
+    ad_p[chip, pl.ds(0, 1), :] = jnp.sum(ad_x[:, pl.ds(0, 1), :], axis=0)
+    for to in chips[1:]:
+        pltpu.make_async_remote_copy(
+            ad_p.at[chip, pl.ds(0, 1)], ad_p.at[chip, pl.ds(0, 1)], s_send.at[2], s_recv.at[2],
+            device_id=(to * 2 + core, x), device_id_type=MESH,
+        ).start()
     send_back(3)
 
-    many(ad_2.at[pl.ds(0, CHIPS * REPS - 1)], s_send.at[1], s_recv.at[1]).wait_recv()
-    total = jnp.sum(ad_2[...], axis=0)
+    sums_plane = many(ad_p.at[pl.ds(0, CHIPS - 1), pl.ds(0, 1)], s_send.at[2], s_recv.at[2])
+    sums_plane.wait_recv()
+    total = jnp.sum(ad_p[:, pl.ds(0, 1), :], axis=0)
     line = lax.broadcasted_iota(jnp.int32, (nblk, 128), 0)
     lane = lax.broadcasted_iota(jnp.int32, (nblk, 128), 1)
-    total = jnp.broadcast_to(total[:1, :], (nblk, 128))
+    total = jnp.broadcast_to(total, (nblk, 128))
     area = width * width
     adam_mean = jnp.sum(jnp.where(lane == line, total, 0.0), axis=1, keepdims=True) / area
     prod_mean = jnp.sum(jnp.where(lane == line + nblk, total, 0.0), axis=1, keepdims=True) / area
@@ -346,15 +329,12 @@
     store_upd = pltpu.make_async_copy(upd, upd_hbm, sem_out.at[1])
     store_upd.start()
 
-    for k in range(REPS):
-        for copy in xc[k]:
-            copy.wait_send()
-        many(f_out.at[k, pl.ds(0, CHIPS - 1)], f_send.at[k], f_recv.at[k]).wait_send()
-        swaps[k].wait_send()
-        trades[k].wait_send()
-    for copy in moments + [sums_chip]:
+    many(xs.at[:, pl.ds(0, 6 * HALF)], x_send.at[0], x_recv.at[0, 0]).wait_send()
+    many(f_out.at[:, pl.ds(0, CHIPS - 1)], f_send.at[0], f_recv.at[0]).wait_send()
+    many(f_out, d_send.at[0], d_recv.at[0]).wait_send()
+    many(ret, p_send.at[0], p_recv.at[0]).wait_send()
+    for copy in (moments, sums_chip, sums_x, sums_plane):
         copy.wait_send()
-    many(ad_2.at[pl.ds(0, CHIPS * REPS - 1)], s_send.at[1], s_recv.at[1]).wait_send()
     many(back.at[pl.ds(0, CHIPS * REPS - 1)], u_send.at[0], u_recv.at[0]).wait_send()
     store_nm.wait()
     store_upd.wait()
@@ -366,6 +346,7 @@
     quarter = width // REPS
     bf, f32 = jnp.bfloat16, jnp.float32
     piece = (rows, quarter)
+    part = (rows, width // CUTS)
     any_spec = pl.BlockSpec(memory_space=pl.ANY)
     vmem = pltpu.VMEM
     dma = pltpu.SemaphoreType.DMA
@@ -382,25 +363,26 @@
             vmem((nblk, rows, quarter), f32),
             vmem((slots, width, width), bf),
             vmem((slots, width, width), bf),
-            vmem((REPS, nblk) + piece, bf),
-            vmem((2, REPS, HALF) + piece, bf),
-            vmem((2, REPS, HALF) + piece, bf),
-            vmem((2, REPS, HALF) + piece, bf),
-            vmem((2, REPS, HALF) + piece, bf),
-            vmem((REPS, PER_PLANE) + piece, bf),
-            vmem((REPS, CHIPS) + piece, bf),
-            vmem((REPS, CHIPS, 2) + piece, bf),
+            vmem((CUTS, nblk) + part, bf),
+            vmem((2, CUTS, HALF) + part, bf),
+            vmem((2, CUTS, HALF) + part, bf),
+            vmem((2, CUTS, HALF) + part, bf),
+            vmem((2, CUTS, HALF) + part, bf),
+            vmem((CUTS, PER_PLANE) + part, bf),
+            vmem((CUTS, CHIPS) + part, bf),
+            vmem((CUTS, CHIPS, 2) + part, bf),
             vmem((width, width), bf),
         ]
         + [vmem((2, CHIPS, 2) + piece, bf)] * REPS
         + [
             vmem((REPS, CHIPS) + piece, bf),
             vmem((REPS * CHIPS,) + piece, bf),
-            vmem((REPS, PER_PLANE) + piece, bf),
+            vmem((REPS, CUTS // REPS, PER_PLANE) + part, bf),
             vmem((nblk,) + piece, f32),
             vmem((nblk,) + piece, bf),
             vmem((16, 128), f32),
-            vmem((REPS * CHIPS, 8, 128), f32),
+            vmem((REPS, 8, 128), f32),
+            vmem((CHIPS, 8, 128), f32),
             vmem((nblk, 128), f32),
             vmem((8, 128), jnp.int32),
             pltpu.SMEM((8, 128), jnp.int32),
@@ -408,11 +390,17 @@
             pltpu.SMEM((8, 128), jnp.int32),
             dma((6,)),
             dma((2,)),
-            dma((REPS * 6,)),
-            dma((REPS * 6,)),
+            dma((1,)),
+            dma((CUTS, 2)),
+            dma((1,)),
+            dma((CUTS,)),
+            dma((1,)),
+            dma((CUTS,)),
+            dma((1,)),
+            dma((REPS,)),
         ]
-        + [dma((REPS,))] * 6
-        + [dma((1,)), dma((1,)), dma((REPS,)), dma((REPS,)), dma((2,)), dma((2,))],
+        + [dma((1,))] * 4
+        + [dma((3,))] * 2,
         compiler_params=pltpu.CompilerParams(
             collective_id=0, has_side_effects=True, vmem_limit_bytes=58 << 20
         ),

time: 70.2 us -> 67.4 us (0.960)
  Pallas kernels: 64.6 us -> 62 us
    pallas_call x1, Pallas kernels: 64.6 us -> 62 us  [one_kernel(): pl.pallas_call(step_kernel, out_shape=(jax.ShapeDtypeStruct((nblk, rows,...]
where the time goes in v3:
time: 67.4 us; the launch traced here: 67.2 us
  Pallas kernels  62 us (92%)
  between operations  1.94 us (3%)
  local copies, waits for them, and re-layouts  1.77 us (3%)
  other arithmetic  1.32 us (2%)
    pallas_call x1, Pallas kernels, one_kernel(): pl.pallas_call(step_kernel, out_shape=(jax.ShapeDtypeStruct((nblk, rows,...  62 us
    unnamed x2, local copies, waits for them, and re-layouts  1.77 us

profile of v3, /device:TPU:1, one launch (start us, length us, event | category | flops | bytes accessed | tf_op | source)
XLA Modules:
  0.0 67.2 jit_solution(12395088650783053130)
XLA Ops:
  0.6 1.3 %fusion.25 = (s32[]{:T(128)}, s32[]{:T(128)}) fusion(s32[32]{0:T(128)} %param.13, s32[32]{0:T(128)} %param.12), kind=kLoop, calls=%fused_computation.35 | loop fusion | flops 286 | bytes 264 | tf_op jit(solution)/shard_map/reduce_sum | solution.py:418
  3.2 62.2 %conditional.1 = ((bf16[32,32,256]{2,1,0:T(8,128)(2,1)S(1)}, f32[32,32,256]{2,1,0:T(8,128)S(1)})) conditional(s32[]{:T(128)} %convert_element_type.27, (bf16[1,32,32,1024]{3,2,1,0:T(8,128)(2,1)}, s32[32]{0:T(128)}, s32[32]{0:T(128)}, f32[32,32,256]{2,1,0:T(8,128)}, bf16[3,1024,1024]{2,1,0:T(8,128)(2,1)}, ...), branch_computations={%region_2.3_spmd, %region_3.7_spmd} | conditional | flops 13163043840 | bytes 251670464 | solution.py:485
  3.3 62.0 %shampoo_step.1 = (bf16[32,32,256]{2,1,0:T(8,128)(2,1)S(1)}, f32[32,32,256]{2,1,0:T(8,128)S(1)}) custom-call(s32[32]{0:T(128)} %get-tuple-element.24.owner, s32[32]{0:T(128)} %get-tuple-element.25.owner_slot, bf16[32,32,1024]{2,1,0:T(8,128)(2,1)} %bitcast.27, f32[32,32,256]{2,1,0:T(8,128)} %get-tuple-element.27.sm_hbm, ...), custom_call_target="tpu_custom_call" | custom-call | flops 4294967296 | bytes 18874368 | tf_op jit(solution)/shard_map/cond/branch_0_fun/shampoo_step/pallas_call | solution.py:353
  65.4 0.8 %copy.79 = bf16[32,32,256]{2,1,0:T(8,128)(2,1)} copy(bf16[32,32,256]{2,1,0:T(8,128)(2,1)S(1)} %get-tuple-element.86) | data formatting | bytes 1048576
  66.2 1.0 %copy.80 = f32[32,32,256]{2,1,0:T(8,128)} copy(f32[32,32,256]{2,1,0:T(8,128)S(1)} %get-tuple-element.87) | data formatting | bytes 2097152

commit v4 on v3

--- a/solution.py
+++ b/solution.py
@@ -202,10 +202,7 @@
         if k >= 2:
             finish(k - 2)
             forward(k - 2)
-    loads[1].wait()
-    left_mul(0)
     swap(1)
-    left_mul(1)
     finish(CUTS - 1)
     forward(CUTS - 1)
 
@@ -217,6 +214,9 @@
         ).start()
     mom_in[x] = summed[pl.ds(x * per_quarter, per_quarter)]
 
+    loads[1].wait()
+    left_mul(0)
+    left_mul(1)
     swap(2)
     left_mul(2)
     loads[2].wait()
@@ -237,10 +237,11 @@
         for i, pb in enumerate(pbs)
     ]
 
-    def send_back(*which):
+    def send_back(*which, some=slice(None)):
         for i in which:
-            trades[i].wait_recv()
-        for to in chips:
+            if some.start is None:
+                trades[i].wait_recv()
+        for to in chips[some]:
             for i in which:
                 if i == 0 and to is chips[0]:
                     back[x * CHIPS + chip] = pbs[i][holder, chip, core]
@@ -255,8 +256,10 @@
     for i in (2, 0, 1, 3):
         squares = right_mul(i, squares)
         trades[i].start()
+        if i == 0:
+            send_back(2)
         if i == 1:
-            send_back(2, 0)
+            send_back(0)
 
     loads[3].wait()
     moments = many(xs.at[0, pl.ds(0, (REPS - 1) * PER_PLANE)], m_send.at[0], m_recv.at[0])
@@ -295,6 +298,7 @@
             device_id=(f, reps[i]), device_id_type=MESH,
         ).start()
     send_back(1)
+    send_back(3, some=slice(None, CHIPS // 2))
     sums_x = many(ad_x.at[pl.ds(0, REPS - 1), pl.ds(0, 1)], s_send.at[1], s_recv.at[1])
     sums_x.wait_recv()
     ad_p[chip, pl.ds(0, 1), :] = jnp.sum(ad_x[:, pl.ds(0, 1), :], axis=0)
@@ -303,7 +307,7 @@
             ad_p.at[chip, pl.ds(0, 1)], ad_p.at[chip, pl.ds(0, 1)], s_send.at[2], s_recv.at[2],
             device_id=(to * 2 + core, x), device_id_type=MESH,
         ).start()
-    send_back(3)
+    send_back(3, some=slice(CHIPS // 2, None))
 
     sums_plane = many(ad_p.at[pl.ds(0, CHIPS - 1), pl.ds(0, 1)], s_send.at[2], s_recv.at[2])
     sums_plane.wait_recv()

time: 67.4 us -> 64.5 us (0.957)
  Pallas kernels: 62 us -> 59.1 us
    pallas_call x1, Pallas kernels: 62 us -> 59.1 us  [one_kernel(): pl.pallas_call(step_kernel, out_shape=(jax.ShapeDtypeStruct((nblk, rows,...]
where the time goes in v4:
time: 64.5 us; the launch traced here: 64.4 us
  Pallas kernels  59.1 us (92%)
  between operations  1.94 us (3%)
  local copies, waits for them, and re-layouts  1.77 us (3%)
  other arithmetic  1.32 us (2%)
    pallas_call x1, Pallas kernels, one_kernel(): pl.pallas_call(step_kernel, out_shape=(jax.ShapeDtypeStruct((nblk, rows,...  59.1 us
    unnamed x2, local copies, waits for them, and re-layouts  1.77 us
    reduce_sum x1, other arithmetic, crowded(): second = jnp.sum(jnp.where(block_slot == 1, other, 0))  1.32 us

profile of v4, /device:TPU:1, one launch (start us, length us, event | category | flops | bytes accessed | tf_op | source)
XLA Modules:
  0.0 64.4 jit_solution(8339094074095842467)
XLA Ops:
  0.6 1.3 %fusion.25 = (s32[]{:T(128)}, s32[]{:T(128)}) fusion(s32[32]{0:T(128)} %param.13, s32[32]{0:T(128)} %param.12), kind=kLoop, calls=%fused_computation.35 | loop fusion | flops 286 | bytes 264 | tf_op jit(solution)/shard_map/reduce_sum | solution.py:422
  3.2 59.3 %conditional.1 = ((bf16[32,32,256]{2,1,0:T(8,128)(2,1)S(1)}, f32[32,32,256]{2,1,0:T(8,128)S(1)})) conditional(s32[]{:T(128)} %convert_element_type.27, (bf16[1,32,32,1024]{3,2,1,0:T(8,128)(2,1)}, s32[32]{0:T(128)}, s32[32]{0:T(128)}, f32[32,32,256]{2,1,0:T(8,128)}, bf16[3,1024,1024]{2,1,0:T(8,128)(2,1)}, ...), branch_computations={%region_2.3_spmd, %region_3.7_spmd} | conditional | flops 13163043840 | bytes 251670464 | solution.py:489
  3.3 59.1 %shampoo_step.1 = (bf16[32,32,256]{2,1,0:T(8,128)(2,1)S(1)}, f32[32,32,256]{2,1,0:T(8,128)S(1)}) custom-call(s32[32]{0:T(128)} %get-tuple-element.24.owner, s32[32]{0:T(128)} %get-tuple-element.25.owner_slot, bf16[32,32,1024]{2,1,0:T(8,128)(2,1)} %bitcast.27, f32[32,32,256]{2,1,0:T(8,128)} %get-tuple-element.27.sm_hbm, ...), custom_call_target="tpu_custom_call" | custom-call | flops 4294967296 | bytes 18874368 | tf_op jit(solution)/shard_map/cond/branch_0_fun/shampoo_step/pallas_call | solution.py:357
  62.6 0.8 %copy.79 = bf16[32,32,256]{2,1,0:T(8,128)(2,1)} copy(bf16[32,32,256]{2,1,0:T(8,128)(2,1)S(1)} %get-tuple-element.86) | data formatting | bytes 1048576
  63.4 1.0 %copy.80 = f32[32,32,256]{2,1,0:T(8,128)} copy(f32[32,32,256]{2,1,0:T(8,128)S(1)} %get-tuple-element.87) | data formatting | bytes 2097152

commit v5 on v4

--- a/solution.py
+++ b/solution.py
@@ -202,9 +202,9 @@
         if k >= 2:
             finish(k - 2)
             forward(k - 2)
-    swap(1)
     finish(CUTS - 1)
     forward(CUTS - 1)
+    swap(1)
 
     for i in range(1, REPS):
         to = reps[i]

time: 64.5 us -> 64.7 us (level)
  no operation moved by 1% of the time
where the time goes in v5:
time: 64.7 us; the launch traced here: 64.5 us
  Pallas kernels  59.3 us (92%)
  between operations  1.94 us (3%)
  local copies, waits for them, and re-layouts  1.77 us (3%)
  other arithmetic  1.32 us (2%)
    pallas_call x1, Pallas kernels, one_kernel(): pl.pallas_call(step_kernel, out_shape=(jax.ShapeDtypeStruct((nblk, rows,...  59.3 us
    unnamed x2, local copies, waits for them, and re-layouts  1.77 us
    reduce_sum x1, other arithmetic, crowded(): second = jnp.sum(jnp.where(block_slot == 1, other, 0))  1.32 us

profile of v5, /device:TPU:1, one launch (start us, length us, event | category | flops | bytes accessed | tf_op | source)
XLA Modules:
  0.0 64.5 jit_solution(4853044429822855231)
XLA Ops:
  0.6 1.3 %fusion.25 = (s32[]{:T(128)}, s32[]{:T(128)}) fusion(s32[32]{0:T(128)} %param.13, s32[32]{0:T(128)} %param.12), kind=kLoop, calls=%fused_computation.35 | loop fusion | flops 286 | bytes 264 | tf_op jit(solution)/shard_map/reduce_sum | solution.py:422
  3.2 59.5 %conditional.1 = ((bf16[32,32,256]{2,1,0:T(8,128)(2,1)S(1)}, f32[32,32,256]{2,1,0:T(8,128)S(1)})) conditional(s32[]{:T(128)} %convert_element_type.27, (bf16[1,32,32,1024]{3,2,1,0:T(8,128)(2,1)}, s32[32]{0:T(128)}, s32[32]{0:T(128)}, f32[32,32,256]{2,1,0:T(8,128)}, bf16[3,1024,1024]{2,1,0:T(8,128)(2,1)}, ...), branch_computations={%region_2.3_spmd, %region_3.7_spmd} | conditional | flops 13163043840 | bytes 251670464 | solution.py:489
  3.3 59.3 %shampoo_step.1 = (bf16[32,32,256]{2,1,0:T(8,128)(2,1)S(1)}, f32[32,32,256]{2,1,0:T(8,128)S(1)}) custom-call(s32[32]{0:T(128)} %get-tuple-element.24.owner, s32[32]{0:T(128)} %get-tuple-element.25.owner_slot, bf16[32,32,1024]{2,1,0:T(8,128)(2,1)} %bitcast.27, f32[32,32,256]{2,1,0:T(8,128)} %get-tuple-element.27.sm_hbm, ...), custom_call_target="tpu_custom_call" | custom-call | flops 4294967296 | bytes 18874368 | tf_op jit(solution)/shard_map/cond/branch_0_fun/shampoo_step/pallas_call | solution.py:357
  62.8 0.8 %copy.79 = bf16[32,32,256]{2,1,0:T(8,128)(2,1)} copy(bf16[32,32,256]{2,1,0:T(8,128)(2,1)S(1)} %get-tuple-element.86) | data formatting | bytes 1048576
  63.6 1.0 %copy.80 = f32[32,32,256]{2,1,0:T(8,128)} copy(f32[32,32,256]{2,1,0:T(8,128)S(1)} %get-tuple-element.87) | data formatting | bytes 2097152

commit v6 on v4

--- a/solution.py
+++ b/solution.py
@@ -19,7 +19,7 @@
 def step_kernel(
     owner, owner_slot, g_hbm, sm_hbm, l_hbm, r_hbm, upd_hbm, nm_hbm,
     grad, sm, left, right, xs, a_in, b_in, c_in, c_out, summed, f_out, g_in,
-    lp, pb0, pb1, pb2, pb3, ret, back, mom_in, nm, upd,
+    lp, held, pb0, pb1, pb2, pb3, ret, back, mom_in, nm, upd,
     ad_1, ad_x, ad_p, factor, place_v, place, inverse_v, inverse,
     sem_in, sem_out, x_send, x_recv, f_send, f_recv, d_send, d_recv,
     p_send, p_recv, u_send, u_recv, m_send, m_recv, s_send, s_recv,
@@ -221,11 +221,26 @@
     left_mul(2)
     loads[2].wait()
     swap(3)
+
+    done = width - quarter
+
+    def columns(i):
+        return pl.ds(pl.multiple_of(reps[i] * quarter, quarter), quarter)
+
+    early = {2: 0, 0: 1}
+    for i, n in early.items():
+        held[n] = jnp.dot(
+            lp[:, :done], right[slot, :done, columns(i)], preferred_element_type=jnp.float32
+        )
     left_mul(3)
 
     def right_mul(i, squares):
-        cols = pl.ds(pl.multiple_of(reps[i] * quarter, quarter), quarter)
-        part = jnp.dot(lp[...], right[slot, :, cols], preferred_element_type=jnp.float32)
+        if i in early:
+            part = held[early[i]] + jnp.dot(
+                lp[:, done:], right[slot, done:, columns(i)], preferred_element_type=jnp.float32
+            )
+        else:
+            part = jnp.dot(lp[...], right[slot, :, columns(i)], preferred_element_type=jnp.float32)
         pbs[i][core] = part.astype(jnp.bfloat16).reshape(CHIPS, 2, rows, quarter)
         return squares + jnp.sum(part * part, axis=0, keepdims=True)
 
@@ -376,6 +391,7 @@
             vmem((CUTS, CHIPS) + part, bf),
             vmem((CUTS, CHIPS, 2) + part, bf),
             vmem((width, width), bf),
+            vmem((2, width, quarter), f32),
         ]
         + [vmem((2, CHIPS, 2) + piece, bf)] * REPS
         + [

time: 64.5 us -> 65.2 us (1.011)
  Pallas kernels: 59.1 us -> 59.8 us
    pallas_call x1, Pallas kernels: 59.1 us -> 59.8 us  [one_kernel(): pl.pallas_call(step_kernel, out_shape=(jax.ShapeDtypeStruct((nblk, rows,...]
where the time goes in v6:
time: 65.2 us; the launch traced here: 65 us
  Pallas kernels  59.8 us (92%)
  between operations  1.94 us (3%)
  local copies, waits for them, and re-layouts  1.77 us (3%)
  other arithmetic  1.32 us (2%)
    pallas_call x1, Pallas kernels, one_kernel(): pl.pallas_call(step_kernel, out_shape=(jax.ShapeDtypeStruct((nblk, rows,...  59.8 us
    unnamed x2, local copies, waits for them, and re-layouts  1.77 us
    reduce_sum x1, other arithmetic, crowded(): second = jnp.sum(jnp.where(block_slot == 1, other, 0))  1.32 us

profile of v6, /device:TPU:1, one launch (start us, length us, event | category | flops | bytes accessed | tf_op | source)
XLA Modules:
  0.0 65.0 jit_solution(18206095806767887769)
XLA Ops:
  0.6 1.3 %fusion.25 = (s32[]{:T(128)}, s32[]{:T(128)}) fusion(s32[32]{0:T(128)} %param.13, s32[32]{0:T(128)} %param.12), kind=kLoop, calls=%fused_computation.35 | loop fusion | flops 286 | bytes 264 | tf_op jit(solution)/shard_map/reduce_sum | solution.py:438
  3.2 60.0 %conditional.1 = ((bf16[32,32,256]{2,1,0:T(8,128)(2,1)S(1)}, f32[32,32,256]{2,1,0:T(8,128)S(1)})) conditional(s32[]{:T(128)} %convert_element_type.27, (bf16[1,32,32,1024]{3,2,1,0:T(8,128)(2,1)}, s32[32]{0:T(128)}, s32[32]{0:T(128)}, f32[32,32,256]{2,1,0:T(8,128)}, bf16[3,1024,1024]{2,1,0:T(8,128)(2,1)}, ...), branch_computations={%region_2.3_spmd, %region_3.7_spmd} | conditional | flops 13163043840 | bytes 251670464 | solution.py:505
  3.3 59.8 %shampoo_step.1 = (bf16[32,32,256]{2,1,0:T(8,128)(2,1)S(1)}, f32[32,32,256]{2,1,0:T(8,128)S(1)}) custom-call(s32[32]{0:T(128)} %get-tuple-element.24.owner, s32[32]{0:T(128)} %get-tuple-element.25.owner_slot, bf16[32,32,1024]{2,1,0:T(8,128)(2,1)} %bitcast.27, f32[32,32,256]{2,1,0:T(8,128)} %get-tuple-element.27.sm_hbm, ...), custom_call_target="tpu_custom_call" | custom-call | flops 4294967296 | bytes 18874368 | tf_op jit(solution)/shard_map/cond/branch_0_fun/shampoo_step/pallas_call | solution.py:372
  63.3 0.8 %copy.79 = bf16[32,32,256]{2,1,0:T(8,128)(2,1)} copy(bf16[32,32,256]{2,1,0:T(8,128)(2,1)S(1)} %get-tuple-element.86) | data formatting | bytes 1048576
  64.1 1.0 %copy.80 = f32[32,32,256]{2,1,0:T(8,128)} copy(f32[32,32,256]{2,1,0:T(8,128)S(1)} %get-tuple-element.87) | data formatting | bytes 2097152

commit v7 on v4

--- a/solution.py
+++ b/solution.py
@@ -38,7 +38,8 @@
     per_quarter = CUTS // REPS
 
     chips = [
-        lax.rem(cy + i // SIDE, SIDE) * SIDE + lax.rem(cz + i % SIDE, SIDE) for i in range(CHIPS)
+        lax.rem(cy + i // SIDE, SIDE) * SIDE + lax.rem(cz + i % SIDE, SIDE)
+        for i in (0, 10, 6, 9, 14, 11, 5, 15, 7, 13, 2, 8, 1, 4, 3, 12)
     ]
     reps = [lax.rem(x + i, REPS) for i in range(REPS)]
 

time: 64.5 us -> 62.2 us (0.964)
  Pallas kernels: 59.1 us -> 56.8 us
    pallas_call x1, Pallas kernels: 59.1 us -> 56.8 us  [one_kernel(): pl.pallas_call(step_kernel, out_shape=(jax.ShapeDtypeStruct((nblk, rows,...]
where the time goes in v7:
time: 62.2 us; the launch traced here: 62.1 us
  Pallas kernels  56.8 us (91%)
  between operations  1.94 us (3%)
  local copies, waits for them, and re-layouts  1.77 us (3%)
  other arithmetic  1.32 us (2%)
    pallas_call x1, Pallas kernels, one_kernel(): pl.pallas_call(step_kernel, out_shape=(jax.ShapeDtypeStruct((nblk, rows,...  56.8 us
    unnamed x2, local copies, waits for them, and re-layouts  1.77 us
    reduce_sum x1, other arithmetic, crowded(): second = jnp.sum(jnp.where(block_slot == 1, other, 0))  1.32 us

profile of v7, /device:TPU:1, one launch (start us, length us, event | category | flops | bytes accessed | tf_op | source)
XLA Modules:
  0.0 62.1 jit_solution(2264856231455775418)
XLA Ops:
  0.6 1.3 %fusion.25 = (s32[]{:T(128)}, s32[]{:T(128)}) fusion(s32[32]{0:T(128)} %param.13, s32[32]{0:T(128)} %param.12), kind=kLoop, calls=%fused_computation.35 | loop fusion | flops 286 | bytes 264 | tf_op jit(solution)/shard_map/reduce_sum | solution.py:423
  3.2 57.1 %conditional.1 = ((bf16[32,32,256]{2,1,0:T(8,128)(2,1)S(1)}, f32[32,32,256]{2,1,0:T(8,128)S(1)})) conditional(s32[]{:T(128)} %convert_element_type.27, (bf16[1,32,32,1024]{3,2,1,0:T(8,128)(2,1)}, s32[32]{0:T(128)}, s32[32]{0:T(128)}, f32[32,32,256]{2,1,0:T(8,128)}, bf16[3,1024,1024]{2,1,0:T(8,128)(2,1)}, ...), branch_computations={%region_2.3_spmd, %region_3.7_spmd} | conditional | flops 13163043840 | bytes 251670464 | solution.py:490
  3.3 56.8 %shampoo_step.1 = (bf16[32,32,256]{2,1,0:T(8,128)(2,1)S(1)}, f32[32,32,256]{2,1,0:T(8,128)S(1)}) custom-call(s32[32]{0:T(128)} %get-tuple-element.24.owner, s32[32]{0:T(128)} %get-tuple-element.25.owner_slot, bf16[32,32,1024]{2,1,0:T(8,128)(2,1)} %bitcast.27, f32[32,32,256]{2,1,0:T(8,128)} %get-tuple-element.27.sm_hbm, ...), custom_call_target="tpu_custom_call" | custom-call | flops 4294967296 | bytes 18874368 | tf_op jit(solution)/shard_map/cond/branch_0_fun/shampoo_step/pallas_call | solution.py:358
  60.3 0.8 %copy.79 = bf16[32,32,256]{2,1,0:T(8,128)(2,1)} copy(bf16[32,32,256]{2,1,0:T(8,128)(2,1)S(1)} %get-tuple-element.86) | data formatting | bytes 1048576
  61.1 1.0 %copy.80 = f32[32,32,256]{2,1,0:T(8,128)} copy(f32[32,32,256]{2,1,0:T(8,128)S(1)} %get-tuple-element.87) | data formatting | bytes 2097152
